TPU v7x, 128 devices: a whole 4x4x4 slice. The times are simulated.
128 devices in a mesh: pipe: 4 (over y), fsdp: 32 (over z, x, core).
Axes of the slice: x: 4, y: 4, z: 4, core: 2. Of those that a mesh axis runs over, the one named last changes fastest.
Arguments:
- tokens: bfloat16 [4096, 4096], P('fsdp'), may hold values from -6 to 6
- targets: bfloat16 [4096, 4096], P('fsdp'), may hold values from -6 to 6
- norm_gain: bfloat16 [4, 4096], P('pipe', 'fsdp'), may hold values from 0.099609375 to 1.8984375
- down_weight: bfloat16 [4, 4096, 256], P('pipe', 'fsdp'), may hold values from -0.09375 to 0.09375
- up_weight: bfloat16 [4, 256, 4096], P('pipe', None, 'fsdp'), may hold values from -0.375 to 0.375
- down_vector: bfloat16 [4, 4096, 256], P('pipe', 'fsdp'), may hold values from -1 to 1
- up_vector: bfloat16 [4, 256, 4096], P('pipe', None, 'fsdp'), may hold values from -1 to 1
Outputs:
- next_down: bfloat16 [4, 4096, 256], P('pipe', 'fsdp')
- next_up: bfloat16 [4, 256, 4096], P('pipe', None, 'fsdp')
- quotient: float32 [], replicated
All inputs are finite; a program needn't handle non-finite values.
Results may differ from a plain program's by a relative error of at most 0.02.
Values may be sent and summed in bfloat16 or wider, within the bound.
No kernel may reach another device: no remote copies, remote signals or barrier semaphores. Data moves between devices by JAX's collectives and lax.ppermute only.
A program may use at most 128 MiB of HBM per device.

v0:
```python
import functools

import jax
import jax.numpy as jnp
from jax import lax
from jax.experimental import pallas as pl
from jax.experimental.pallas import tpu as pltpu
from jax.sharding import Mesh, PartitionSpec as P

EPS = 1e-06
D = 4096
RANK = 256
LAYERS = 4
TOKENS = 4096
ROWS = 64
HALF = 2048
F32 = jnp.float32
BF16 = jnp.bfloat16


def shift(value, axis, steps):
    return lax.ppermute(value, axis, [(i, (i + steps) % 4) for i in range(4)])


def swap(value):
    return lax.ppermute(value, "c", [(0, 1), (1, 0)])


def dot(left, right, dims):
    return lax.dot_general(left, right, (dims, ((), ())), preferred_element_type=F32)


def mm(left, right):
    return dot(left, right, ((1,), (0,)))


def mm_nt(left, right):
    return dot(left, right, ((1,), (1,)))


def mm_tn(left, right):
    return dot(left, right, ((0,), (0,)))


def core_rows(tokens, core):
    rows = lax.dynamic_slice_in_dim(tokens, lax.axis_index("y") * 32, 32, 0)
    rows = rows.reshape(32, 16, 2, 128)
    own = lax.dynamic_index_in_dim(rows, core, 2, keepdims=False).reshape(32, HALF)
    other = lax.dynamic_index_in_dim(rows, 1 - core, 2, keepdims=False).reshape(32, HALF)
    got = swap(other)
    first = jnp.where(core == 0, own, got)
    second = jnp.where(core == 0, got, own)
    return jnp.concatenate([first, second], 0)


def middle(full):
    u, v = full[:, :256], full[:, 256:512]
    r = lax.rsqrt(full[:, 512:513] * (1.0 / D) + EPS)
    c = full[:, 639:640] * (1.0 / D)
    r3c = r * r * r * c
    pre = r * u
    pre_dot = r * v - r3c * u
    s = jax.nn.sigmoid(pre)
    slope = s * (1.0 + pre * (1.0 - s))
    slope2 = s * (1.0 - s) * (2.0 + pre * (1.0 - 2.0 * s))
    act = (pre * s).astype(BF16)
    act_dot = (slope * pre_dot).astype(BF16)
    return u, v, r, c, pre_dot, slope, slope2, act, act_dot


def inner_cotangents(mid, e_full):
    e, e_dot = e_full[:, :256], e_full[:, 256:]
    pre_dot, slope, slope2 = mid[4], mid[5], mid[6]
    s = (e * slope).astype(BF16)
    s_dot = (e_dot * slope + e * slope2 * pre_dot).astype(BF16)
    return s, s_dot


def fetches(w_ref, layer, first, buf, sems):
    return [
        pltpu.make_async_copy(
            w_ref.at[layer, pl.ds(4 * i, 4), pl.ds(first, 2)],
            buf.at[pl.ds(4 * i, 4)],
            sems.at[i],
        )
        for i in range(4)
    ]


def pick(buf, i, which):
    return buf[4 * i : 4 * i + 4, which].reshape(512, RANK)


def write_sums(part_ref, u, v, s1, s2):
    lane = lax.broadcasted_iota(jnp.int32, (ROWS, 128), 1)
    part_ref[:, :256] = u
    part_ref[:, 256:512] = v
    part_ref[:, 512:] = jnp.where(lane < 64, s1, s2)


def first_kernel(x_ref, w_ref, part_ref, buf, sems):
    copies = fetches(w_ref, 0, 0, buf, sems)
    for copy in copies:
        copy.start()
    u = jnp.zeros((ROWS, RANK), F32)
    v = jnp.zeros((ROWS, RANK), F32)
    s1 = jnp.zeros((ROWS, 1), F32)
    for i in range(4):
        h = x_ref[:ROWS, 512 * i : 512 * i + 512]
        hf = h.astype(F32)
        s1 += jnp.sum(hf * hf, axis=1, keepdims=True)
        copies[i].wait()
        u += mm(h, pick(buf, i, 0))
        v += mm(h, pick(buf, i, 1))
    write_sums(part_ref, u, v, s1, jnp.zeros((ROWS, 1), F32))


def forward_kernel(
    layer, x_ref, own_ref, got_ref, w_ref, xo_ref, part_ref, buf0, buf1, sems0, sems1
):
    ends = fetches(w_ref, layer - 1, 2, buf0, sems0)
    starts = fetches(w_ref, layer, 0, buf1, sems1)
    for i in range(4):
        ends[i].start()
        starts[i].start()
    mid = middle(own_ref[...] + got_ref[...])
    act, act_dot = mid[7], mid[8]
    pair = jnp.concatenate([act, act_dot], 0)
    both = jnp.zeros((2 * ROWS, RANK), F32)
    cross = jnp.zeros((ROWS, RANK), F32)
    s1 = jnp.zeros((ROWS, 1), F32)
    s2 = jnp.zeros((ROWS, 1), F32)
    for i in range(4):
        cols = slice(512 * i, 512 * i + 512)
        ends[i].wait()
        step = mm_nt(pair, pick(buf0, i, 0))
        tail = mm_nt(act, pick(buf0, i, 1))
        h = (x_ref[:ROWS, cols].astype(F32) + step[:ROWS]).astype(BF16)
        t = (x_ref[ROWS:, cols].astype(F32) + step[ROWS:] + tail).astype(BF16)
        xo_ref[:ROWS, cols] = h
        xo_ref[ROWS:, cols] = t
        hf, tf = h.astype(F32), t.astype(F32)
        s1 += jnp.sum(hf * hf, axis=1, keepdims=True)
        s2 += jnp.sum(hf * tf, axis=1, keepdims=True)
        starts[i].wait()
        both += mm(jnp.concatenate([h, t], 0), pick(buf1, i, 0))
        cross += mm(h, pick(buf1, i, 1))
    write_sums(part_ref, both[:ROWS], both[ROWS:] + cross, s1, s2)


def seed_kernel(x_ref, own_ref, got_ref, goal_ref, w_ref, cot_ref, part_ref, buf, sems):
    ends = fetches(w_ref, LAYERS - 1, 2, buf, sems)
    for copy in ends:
        copy.start()
    mid = middle(own_ref[...] + got_ref[...])
    act, act_dot = mid[7], mid[8]
    pair = jnp.concatenate([act, act_dot], 0)
    both = jnp.zeros((2 * ROWS, RANK), F32)
    cross = jnp.zeros((ROWS, RANK), F32)
    for i in range(4):
        cols = slice(512 * i, 512 * i + 512)
        ends[i].wait()
        b, q = pick(buf, i, 0), pick(buf, i, 1)
        step = mm_nt(pair, b)
        tail = mm_nt(act, q)
        h = (x_ref[:ROWS, cols].astype(F32) + step[:ROWS]).astype(BF16)
        t = (x_ref[ROWS:, cols].astype(F32) + step[ROWS:] + tail).astype(BF16)
        d = (h.astype(F32) - goal_ref[:, cols].astype(F32)).astype(BF16)
        cot_ref[:ROWS, cols] = d
        cot_ref[ROWS:, cols] = t
        both += mm(jnp.concatenate([d, t], 0), b)
        cross += mm(d, q)
    part_ref[:, :256] = both[:ROWS]
    part_ref[:, 256:] = both[ROWS:] + cross


def backward_kernel(
    layer,
    x_ref,
    cot_ref,
    own_ref,
    got_ref,
    e_own_ref,
    e_got_ref,
    w_ref,
    out_ref,
    part_ref,
    buf0,
    buf1,
    sems0,
    sems1,
):
    ends = fetches(w_ref, layer, 0, buf0, sems0)
    starts = fetches(w_ref, layer - 1, 2, buf1, sems1)
    for i in range(4):
        ends[i].start()
        starts[i].start()
    mid = middle(own_ref[...] + got_ref[...])
    u, v, r, c = mid[:4]
    s, s_dot = inner_cotangents(mid, e_own_ref[...] + e_got_ref[...])
    pair = jnp.concatenate([s, s_dot], 0)
    sf, sdf = s.astype(F32), s_dot.astype(F32)
    mean = jnp.sum(sf * u, axis=1, keepdims=True) * (1.0 / D)
    mean_dot = jnp.sum(sf * v + sdf * u, axis=1, keepdims=True) * (1.0 / D)
    r3 = r * r * r
    r3c = r3 * c
    r3m = r3 * mean
    by_h = 3.0 * r3m * r * r * c - r3 * mean_dot
    both = jnp.zeros((2 * ROWS, RANK), F32)
    cross = jnp.zeros((ROWS, RANK), F32)
    for i in range(4):
        cols = slice(512 * i, 512 * i + 512)
        ends[i].wait()
        ms = mm_nt(pair, pick(buf0, i, 0))
        m = ms[:ROWS]
        m_dot = ms[ROWS:] + mm_nt(s, pick(buf0, i, 1))
        h, t = x_ref[:ROWS, cols].astype(F32), x_ref[ROWS:, cols].astype(F32)
        bar = r * m - r3m * h
        bar_dot = r * m_dot - r3c * m - r3m * t + by_h * h
        d = (cot_ref[:ROWS, cols].astype(F32) + bar).astype(BF16)
        d_dot = (cot_ref[ROWS:, cols].astype(F32) + bar_dot).astype(BF16)
        out_ref[:ROWS, cols] = d
        out_ref[ROWS:, cols] = d_dot
        starts[i].wait()
        both += mm(jnp.concatenate([d, d_dot], 0), pick(buf1, i, 0))
        cross += mm(d, pick(buf1, i, 1))
    part_ref[:, :256] = both[:ROWS]
    part_ref[:, 256:] = both[ROWS:] + cross


def hessian_kernel(place_ref, *refs):
    inputs, downs, ups = refs[:12], refs[12:16], refs[16:20]
    me_z, me_x = place_ref[0], place_ref[1]
    for i in range(2):
        x_ref, cot_ref, own_ref, got_ref, e_own_ref, e_got_ref = inputs[6 * i : 6 * i + 6]
        mid = middle(own_ref[...] + got_ref[...])
        r, c, act, act_dot = mid[2], mid[3], mid[7], mid[8]
        r3c = r * r * r * c
        s, s_dot = inner_cotangents(mid, e_own_ref[...] + e_got_ref[...])
        pair = jnp.concatenate([s, s_dot], 0)
        acts = jnp.concatenate([act_dot, act], 0)
        for slot_z, far_z in enumerate((0, 1, 3, 2)):
            for slot_x, far_x in enumerate((0, 1, 3, 2)):
                block = ((me_z + far_z) & 3) * 4 + ((me_x + far_x) & 3)
                cols = pl.ds(pl.multiple_of(block * 128, 128), 128)
                x = x_ref[:, cols].astype(F32)
                h, t = x[:ROWS], x[ROWS:]
                normed = jnp.concatenate(
                    [(r * t - r3c * h).astype(BF16), (r * h).astype(BF16)], 0
                )
                downs[slot_z][slot_x, i] = mm_tn(normed, pair).astype(BF16)
                ups[slot_x][slot_z, i] = mm_tn(cot_ref[:, cols], acts).astype(BF16)


VMEM = pl.BlockSpec(memory_space=pltpu.VMEM)
ANY = pl.BlockSpec(memory_space=pl.ANY)
SMEM = pl.BlockSpec(memory_space=pltpu.SMEM)
BUF = pltpu.VMEM((16, 2, 128, RANK), BF16)
SEMS = pltpu.SemaphoreType.DMA((4,))


def shape(dims, dtype):
    return jax.ShapeDtypeStruct(dims, dtype)


def call(kernel, in_specs, outs, scratch, flops, moved):
    return pl.pallas_call(
        kernel,
        in_specs=in_specs,
        out_specs=[VMEM] * len(outs),
        out_shape=outs,
        scratch_shapes=scratch,
        compiler_params=pltpu.CompilerParams(vmem_limit_bytes=40 * 1024 * 1024),
        cost_estimate=pl.CostEstimate(flops=flops, bytes_accessed=moved, transcendentals=0),
    )


def direct_scatter(slots, axis):
    own, ahead, behind, across = slots
    return (
        own.astype(F32)
        + shift(ahead, axis, 1).astype(F32)
        + shift(behind, axis, -1).astype(F32)
        + shift(across, axis, 2).astype(F32)
    )


def slots_of(value, axis_name, dim):
    me = lax.axis_index(axis_name)
    return [
        lax.dynamic_index_in_dim(value, (me + step) % 4, dim, keepdims=False)
        for step in (0, 1, 3, 2)
    ]


def sum_all(value):
    value = value + swap(value)
    for axis in ("x", "z", "y"):
        value = value + shift(value, axis, 1) + shift(value, axis, -1) + shift(value, axis, 2)
    return value


def local(tokens, targets, norm_gain, down_weight, up_weight, down_vector, up_vector):
    core = lax.axis_index("c")
    gain = norm_gain[0].astype(F32)[:, None]
    chunk = jnp.stack(
        [
            (down_weight[0].astype(F32) * gain).astype(BF16),
            (down_vector[0].astype(F32) * gain).astype(BF16),
            up_weight[0].T,
            up_vector[0].T,
        ]
    )[None]
    gathered = lax.all_gather(chunk, ("y", "z", "x"), axis=0, tiled=True)
    gathered = gathered.reshape(LAYERS, 16, 4, 128, RANK)
    h = core_rows(tokens, core)
    goal = core_rows(targets, core)
    x = jnp.concatenate([h, jnp.zeros_like(h)], 0)
    place = jnp.stack([lax.axis_index("z"), lax.axis_index("x")]).astype(jnp.int32)
    wide = shape((2 * ROWS, HALF), BF16)
    sums = shape((ROWS, 640), F32)
    e_sums = shape((ROWS, 512), F32)
    work = 6 * 2 * ROWS * HALF * RANK

    def exchanged(part):
        return part, swap(part)

    states, sides, cots, e_sides = [x], [], {}, {}
    (part,) = call(first_kernel, [VMEM, ANY], [sums], [BUF, SEMS], work // 3, 3 << 20)(x, gathered)
    sides.append(exchanged(part))
    for layer in range(1, LAYERS):
        x, part = call(
            functools.partial(forward_kernel, layer),
            [VMEM, VMEM, VMEM, ANY],
            [wide, sums],
            [BUF, BUF, SEMS, SEMS],
            work,
            5 << 20,
        )(x, *sides[-1], gathered)
        states.append(x)
        sides.append(exchanged(part))
    cot, part = call(
        seed_kernel,
        [VMEM, VMEM, VMEM, VMEM, ANY],
        [wide, e_sums],
        [BUF, SEMS],
        work,
        3 << 20,
    )(x, *sides[-1], goal, gathered)

    slot = shape((4, 2, 128, RANK), BF16)
    shares = [None, None]
    for layer in reversed(range(LAYERS)):
        cots[layer] = cot
        e_sides[layer] = exchanged(part)
        if layer > 0:
            cot, part = call(
                functools.partial(backward_kernel, layer),
                [VMEM] * 6 + [ANY],
                [wide, e_sums],
                [BUF, BUF, SEMS, SEMS],
                work,
                5 << 20,
            )(states[layer], cot, *sides[layer], *e_sides[layer], gathered)
        if layer in (2, 0):
            operands = []
            for one in (layer, layer + 1):
                operands += [states[one], cots[one], *sides[one], *e_sides[one]]
            blocks = call(
                hessian_kernel, [SMEM] + [VMEM] * 12, [slot] * 8, [], 2 * work, 6 << 20
            )(place, *operands)
            down = direct_scatter(blocks[:4], "z").astype(BF16)
            up = direct_scatter(blocks[4:], "x").astype(BF16)
            down = direct_scatter(list(down), "x").astype(BF16)
            up = direct_scatter(list(up), "z").astype(BF16)
            shares[layer // 2] = jnp.concatenate([down, up], 1)

    both = jnp.concatenate([shares[0], shares[1]], 0)
    share = direct_scatter(slots_of(both, "y", 0), "y")
    share_down = share[:128] * gain
    share_up = share[128:].T
    own_down = down_vector[0].astype(F32)
    own_up = up_vector[0].astype(F32)
    totals = jnp.stack(
        [
            jnp.sum(share_down * share_down) + jnp.sum(share_up * share_up),
            jnp.sum(own_down * share_down) + jnp.sum(own_up * share_up),
            jnp.sum(own_down * own_down) + jnp.sum(own_up * own_up),
        ]
    )
    totals = sum_all(totals)
    total_count = 2.0 * LAYERS * D * RANK
    square_mean = totals[0] / total_count
    cross_mean = totals[1] / total_count
    vector_mean = totals[2] / total_count
    scale_rms = jnp.sqrt(square_mean + EPS)
    quotient = cross_mean / (vector_mean + EPS) / TOKENS
    next_down = (share_down / scale_rms).astype(BF16)[None]
    next_up = (share_up / scale_rms).astype(BF16)[None]
    return (next_down, next_up, quotient)


def solution(mesh):
    fine = Mesh(mesh.devices.reshape(4, 4, 4, 2), ("y", "z", "x", "c"))
    fsdp = ("z", "x", "c")
    placed = (
        P(fsdp, None),
        P(fsdp, None),
        P("y", fsdp),
        P("y", fsdp, None),
        P("y", None, fsdp),
        P("y", fsdp, None),
        P("y", None, fsdp),
    )
    return jax.shard_map(
        local,
        mesh=fine,
        in_specs=placed,
        out_specs=(P("y", fsdp, None), P("y", None, fsdp), P()),
        check_vma=False,
    )
```

profile of v0, /device:TPU:1, one launch (start us, length us, event | category | flops | bytes accessed | tf_op | source)
XLA Modules:
  0.0 317.8 jit_solution(18296179739098370382)
XLA Ops:
  17.0 102.3 %all-gather.3.cloned.1.call-done = bf16[256,128,256]{2,1,0:T(8,128)(2,1)} async-done(((bf16[4,128,256]{2,1,0:T(8,128)(2,1)}), bf16[256,128,256]{2,1,0:T(8,128)(2,1)}) %all-gather.3.cloned.1.call-update) | async-done | bytes 16777232 | tf_op jit(solution)/shard_map/all_gather | solution.py:314
  122.8 3.6 %shard_map.95 = (bf16[128,2048]{1,0:T(8,128)(2,1)S(1)}, f32[64,640]{1,0:T(8,128)S(1)}) custom-call(bf16[128,2048]{1,0:T(8,128)(2,1)S(1)} %maximum_maximum_fusion.x_ref.refs_0_, f32[64,640]{1,0:T(8,128)S(1)} %shard_map.94.own_ref.refs_2_, f32[64,640]{1,0:T(8,128)S(1)} %collective-permute-done.1.got_ref.refs_3_, bf16[4,16,4,128,256]{4,3,2,1,0:T(8,128)(2,1)} %bitcast.117), custom_call_target="tpu_custom_call" | custom-call | flops 402653184 | bytes 5242880 | tf_op jit(solution)/shard_map/pallas_call | solution.py:332
  128.9 3.7 %shard_map.96 = (bf16[128,2048]{1,0:T(8,128)(2,1)S(1)}, f32[64,640]{1,0:T(8,128)S(1)}) custom-call(bf16[128,2048]{1,0:T(8,128)(2,1)S(1)} %get-tuple-element.33.x_ref.refs_6_, f32[64,640]{1,0:T(8,128)S(1)} %get-tuple-element.34.own_ref.refs_8_, f32[64,640]{1,0:T(8,128)S(1)} %collective-permute-done.2.got_ref.refs_9_, bf16[4,16,4,128,256]{4,3,2,1,0:T(8,128)(2,1)} %bitcast.118), custom_call_target="tpu_custom_call" | custom-call | flops 402653184 | bytes 5242880 | tf_op jit(solution)/shard_map/pallas_call | solution.py:332
  134.1 3.7 %shard_map.97 = (bf16[128,2048]{1,0:T(8,128)(2,1)S(1)}, f32[64,640]{1,0:T(8,128)S(1)}) custom-call(bf16[128,2048]{1,0:T(8,128)(2,1)S(1)} %get-tuple-element.35.x_ref.refs_0_, f32[64,640]{1,0:T(8,128)S(1)} %get-tuple-element.36.own_ref.refs_2_, f32[64,640]{1,0:T(8,128)S(1)} %collective-permute-done.3.got_ref.refs_3_, bf16[4,16,4,128,256]{4,3,2,1,0:T(8,128)(2,1)} %bitcast.119), custom_call_target="tpu_custom_call" | custom-call | flops 402653184 | bytes 5242880 | tf_op jit(solution)/shard_map/pallas_call | solution.py:332
  139.2 3.0 shard_map.98
  143.9 4.0 %shard_map.99 = (bf16[128,2048]{1,0:T(8,128)(2,1)S(1)}, f32[64,512]{1,0:T(8,128)}) custom-call(bf16[128,2048]{1,0:T(8,128)(2,1)S(1)} %get-tuple-element.37.x_ref.refs_6_, bf16[128,2048]{1,0:T(8,128)(2,1)S(1)} %get-tuple-element.39.cot_ref.refs_7_, f32[64,640]{1,0:T(8,128)S(1)} %get-tuple-element.38.own_ref.refs_8_, ...), custom_call_target="tpu_custom_call" | custom-call | flops 402653184 | bytes 5242880 | tf_op jit(solution)/shard_map/pallas_call | solution.py:357
  155.2 2.5 shard_map.103
  161.4 4.3 %shard_map.100 = (bf16[128,2048]{1,0:T(8,128)(2,1)S(1)}, f32[64,512]{1,0:T(8,128)S(1)}) custom-call(bf16[128,2048]{1,0:T(8,128)(2,1)S(1)} %get-tuple-element.35.x_ref.refs_0_, bf16[128,2048]{1,0:T(8,128)(2,1)S(1)} %get-tuple-element.41.cot_ref.refs_1_, f32[64,640]{1,0:T(8,128)S(1)} %copy-done.3, f32[64,640]{1,0:T(8,128)S(1)} %copy-done.5, ...), custom_call_target="tpu_custom_call" | custom-call | flops 402653184 | bytes 5242880 | tf_op jit(solution)/shard_map/pallas_call | solution.py:357
  170.3 3.3 %shard_map.101 = (bf16[128,2048]{1,0:T(8,128)(2,1)S(1)}, f32[64,512]{1,0:T(8,128)S(1)}) custom-call(bf16[128,2048]{1,0:T(8,128)(2,1)S(1)} %get-tuple-element.33.x_ref.refs_6_, bf16[128,2048]{1,0:T(8,128)(2,1)S(1)} %get-tuple-element.43.cot_ref.refs_7_, f32[64,640]{1,0:T(8,128)S(1)} %get-tuple-element.34.own_ref.refs_8_, f32[64,640]{1,0:T(8,128)S(1)} %copy-done.1, ...), custom_call_target="tpu_custom_call" | custom-call | flops 402653184 | bytes 5242880 | tf_op jit(solution)/shard_map/pallas_call | solution.py:357
  174.8 9.0 %collective-permute-start.9 = (f32[64,512]{1,0:T(8,128)S(1)}, f32[64,512]{1,0:T(8,128)S(1)}, u32[]{:S(2)}, u32[]{:S(2)}) collective-permute-start(f32[64,512]{1,0:T(8,128)S(1)} %get-tuple-element.46.refs_4_), channel_id=1, source_target_pairs={{0,1},{1,0},{2,3},{3,2},{4,5},{5,4},{6,7},{7,6},{8,9},{9,8},{10,11... | collective-permute-start | bytes 393224 | tf_op jit(solution)/shard_map/ppermute | solution.py:26
  189.0 4.8 %collective-permute-done.30 = bf16[4,2,128,256]{3,2,1,0:T(8,128)(2,1)S(1)} collective-permute-done((bf16[4,2,128,256]{3,2,1,0:T(8,128)(2,1)S(1)}, bf16[4,2,128,256]{3,2,1,0:T(8,128)(2,1)S(1)}, u32[]{:S(2)}, u32[]{:S(2)}) %collective-permute-start.30) | collective-permute-done | bytes 524320 | tf_op jit(solution)/shard_map/ppermute | solution.py:22
  195.4 3.1 shard_map.102
  207.4 20.1 %collective-permute-done.32 = bf16[2,128,256]{2,1,0:T(8,128)(2,1)S(1)} collective-permute-done((bf16[2,128,256]{2,1,0:T(8,128)(2,1)}, bf16[2,128,256]{2,1,0:T(8,128)(2,1)S(1)}, u32[]{:S(2)}, u32[]{:S(2)}) %collective-permute-start.32) | collective-permute-done | bytes 131104 | tf_op jit(solution)/shard_map/ppermute | solution.py:22
  233.3 2.6 collective-permute-start.14
  235.8 5.1 %collective-permute-done.16 = bf16[4,2,128,256]{3,2,1,0:T(8,128)(2,1)S(1)} collective-permute-done((bf16[4,2,128,256]{3,2,1,0:T(8,128)(2,1)}, bf16[4,2,128,256]{3,2,1,0:T(8,128)(2,1)S(1)}, u32[]{:S(2)}, u32[]{:S(2)}) %collective-permute-start.16) | collective-permute-done | bytes 524320 | tf_op jit(solution)/shard_map/ppermute | solution.py:22
  240.9 5.6 %collective-permute-done.18 = bf16[4,2,128,256]{3,2,1,0:T(8,128)(2,1)S(1)} collective-permute-done((bf16[4,2,128,256]{3,2,1,0:T(8,128)(2,1)S(1)}, bf16[4,2,128,256]{3,2,1,0:T(8,128)(2,1)S(1)}, u32[]{:S(2)}, u32[]{:S(2)}) %collective-permute-start.18) | collective-permute-done | bytes 524320 | tf_op jit(solution)/shard_map/ppermute | solution.py:22
  253.0 2.3 collective-permute-done.21
  255.9 3.8 %collective-permute-start.35 = (bf16[256,256]{1,0:T(8,128)(2,1)S(1)}, bf16[256,256]{1,0:T(8,128)(2,1)S(1)}, u32[]{:S(2)}, u32[]{:S(2)}) collective-permute-start(bf16[256,256]{1,0:T(8,128)(2,1)S(1)} %get-tuple-element.87), channel_id=1, source_target_pairs={{0,96},{32,0},{64,32},{96,64},{1,97},{33,1},{65,33},{97,65},{2,98}... | collective-permute-start | bytes 393224 | tf_op jit(solution)/shard_map/ppermute | solution.py:22
  262.2 2.7 collective-permute-done.36
  271.3 13.3 %collective-permute-start.37 = (f32[3]{0:T(128)S(1)}, f32[3]{0:T(128)S(1)}, u32[]{:S(2)}, u32[]{:S(2)}) collective-permute-start(f32[3]{0:T(128)S(1)} %pad_maximum_fusion.2), channel_id=1, source_target_pairs={{0,1},{1,0},{2,3},{3,2},{4,5},{5,4},{6,7},{7,6},{8,9},{9,8},{10,11... | collective-permute-start | bytes 44 | tf_op jit(solution)/shard_map/ppermute | solution.py:26
  289.8 2.8 collective-permute-done.40
  296.7 2.4 collective-permute-done.43
  299.5 2.3 collective-permute-start.45
  302.8 3.0 collective-permute-done.46
  (166 shorter events, 83.1 us)
Async XLA Ops:
  7.2 112.1 %all-gather.3.cloned.1.call-start = ((), (), s32[]{:S(2)}) async-start(), calls=%async_computation | async-start | bytes 17039360 | tf_op jit(solution)/shard_map/all_gather | solution.py:314
  157.7 16.0 %collective-permute-start.22 = (bf16[4,2,128,256]{3,2,1,0:T(8,128)(2,1)S(1)}, bf16[4,2,128,256]{3,2,1,0:T(8,128)(2,1)S(1)}, u32[]{:S(2)}, u32[]{:S(2)}) collective-permute-start(bf16[4,2,128,256]{3,2,1,0:T(8,128)(2,1)S(1)} %get-tuple-element.56), channel_id=1, source_target_pairs={{0,8},{8,16},{16,24},{24,0},{1,9},{9,17},{17,25},{25,1},{2,10},{10... | collective-permute-start | bytes 1572872 | tf_op jit(solution)/shard_map/ppermute | solution.py:22
  158.3 16.5 %collective-permute-start.23 = (bf16[4,2,128,256]{3,2,1,0:T(8,128)(2,1)S(1)}, bf16[4,2,128,256]{3,2,1,0:T(8,128)(2,1)S(1)}, u32[]{:S(2)}, u32[]{:S(2)}) collective-permute-start(bf16[4,2,128,256]{3,2,1,0:T(8,128)(2,1)S(1)} %get-tuple-element.57), channel_id=1, source_target_pairs={{0,24},{8,0},{16,8},{24,16},{1,25},{9,1},{17,9},{25,17},{2,26},{10... | collective-permute-start | bytes 1572872 | tf_op jit(solution)/shard_map/ppermute | solution.py:22
  160.5 23.4 %collective-permute-start.24 = (bf16[4,2,128,256]{3,2,1,0:T(8,128)(2,1)S(1)}, bf16[4,2,128,256]{3,2,1,0:T(8,128)(2,1)S(1)}, u32[]{:S(2)}, u32[]{:S(2)}) collective-permute-start(bf16[4,2,128,256]{3,2,1,0:T(8,128)(2,1)S(1)} %get-tuple-element.58), channel_id=1, source_target_pairs={{0,16},{8,24},{16,0},{24,8},{1,17},{9,25},{17,1},{25,9},{2,18},{10... | collective-permute-start | bytes 1572872 | tf_op jit(solution)/shard_map/ppermute | solution.py:22
  167.0 19.1 %collective-permute-start.28 = (bf16[4,2,128,256]{3,2,1,0:T(8,128)(2,1)S(1)}, bf16[4,2,128,256]{3,2,1,0:T(8,128)(2,1)S(1)}, u32[]{:S(2)}, u32[]{:S(2)}) collective-permute-start(bf16[4,2,128,256]{3,2,1,0:T(8,128)(2,1)S(1)} %get-tuple-element.60), channel_id=1, source_target_pairs={{0,2},{2,4},{4,6},{6,0},{1,3},{3,5},{5,7},{7,1},{8,10},{10,12},{12... | collective-permute-start | bytes 1572872 | tf_op jit(solution)/shard_map/ppermute | solution.py:22
  168.2 19.4 %collective-permute-start.29 = (bf16[4,2,128,256]{3,2,1,0:T(8,128)(2,1)S(1)}, bf16[4,2,128,256]{3,2,1,0:T(8,128)(2,1)S(1)}, u32[]{:S(2)}, u32[]{:S(2)}) collective-permute-start(bf16[4,2,128,256]{3,2,1,0:T(8,128)(2,1)S(1)} %get-tuple-element.61), channel_id=1, source_target_pairs={{0,6},{2,0},{4,2},{6,4},{1,7},{3,1},{5,3},{7,5},{8,14},{10,8},{12,... | collective-permute-start | bytes 1572872 | tf_op jit(solution)/shard_map/ppermute | solution.py:22
  173.7 20.2 %collective-permute-start.30 = (bf16[4,2,128,256]{3,2,1,0:T(8,128)(2,1)S(1)}, bf16[4,2,128,256]{3,2,1,0:T(8,128)(2,1)S(1)}, u32[]{:S(2)}, u32[]{:S(2)}) collective-permute-start(bf16[4,2,128,256]{3,2,1,0:T(8,128)(2,1)S(1)} %get-tuple-element.62), channel_id=1, source_target_pairs={{0,4},{2,6},{4,0},{6,2},{1,5},{3,7},{5,1},{7,3},{8,12},{10,14},{12... | collective-permute-start | bytes 1572872 | tf_op jit(solution)/shard_map/ppermute | solution.py:22
  174.8 20.5 %collective-permute-start.9 = (f32[64,512]{1,0:T(8,128)S(1)}, f32[64,512]{1,0:T(8,128)S(1)}, u32[]{:S(2)}, u32[]{:S(2)}) collective-permute-start(f32[64,512]{1,0:T(8,128)S(1)} %get-tuple-element.46.refs_4_), channel_id=1, source_target_pairs={{0,1},{1,0},{2,3},{3,2},{4,5},{5,4},{6,7},{7,6},{8,9},{9,8},{10,11... | collective-permute-start | bytes 393224 | tf_op jit(solution)/shard_map/ppermute | solution.py:26
  184.9 16.6 %collective-permute-start.25 = (bf16[2,128,256]{2,1,0:T(8,128)(2,1)S(1)}, bf16[2,128,256]{2,1,0:T(8,128)(2,1)}, u32[]{:S(2)}, u32[]{:S(2)}) collective-permute-start(bf16[2,128,256]{2,1,0:T(8,128)(2,1)S(1)} %get-tuple-element.94), channel_id=1, source_target_pairs={{0,2},{2,4},{4,6},{6,0},{1,3},{3,5},{5,7},{7,1},{8,10},{10,12},{12... | collective-permute-start | bytes 393224 | tf_op jit(solution)/shard_map/ppermute | solution.py:22
  186.0 16.8 %collective-permute-start.26 = (bf16[2,128,256]{2,1,0:T(8,128)(2,1)S(1)}, bf16[2,128,256]{2,1,0:T(8,128)(2,1)}, u32[]{:S(2)}, u32[]{:S(2)}) collective-permute-start(bf16[2,128,256]{2,1,0:T(8,128)(2,1)S(1)} %get-tuple-element.96), channel_id=1, source_target_pairs={{0,6},{2,0},{4,2},{6,4},{1,7},{3,1},{5,3},{7,5},{8,14},{10,8},{12,... | collective-permute-start | bytes 393224 | tf_op jit(solution)/shard_map/ppermute | solution.py:22
  187.5 16.2 %collective-permute-start.27 = (bf16[2,128,256]{2,1,0:T(8,128)(2,1)}, bf16[2,128,256]{2,1,0:T(8,128)(2,1)}, u32[]{:S(2)}, u32[]{:S(2)}) collective-permute-start(bf16[2,128,256]{2,1,0:T(8,128)(2,1)} %get-tuple-element.95), channel_id=1, source_target_pairs={{0,4},{2,6},{4,0},{6,2},{1,5},{3,7},{5,1},{7,3},{8,12},{10,14},{12... | collective-permute-start | bytes 393224 | tf_op jit(solution)/shard_map/ppermute | solution.py:22
  195.0 10.4 %collective-permute-start.31 = (bf16[2,128,256]{2,1,0:T(8,128)(2,1)}, bf16[2,128,256]{2,1,0:T(8,128)(2,1)}, u32[]{:S(2)}, u32[]{:S(2)}) collective-permute-start(bf16[2,128,256]{2,1,0:T(8,128)(2,1)} %get-tuple-element.97), channel_id=1, source_target_pairs={{0,8},{8,16},{16,24},{24,0},{1,9},{9,17},{17,25},{25,1},{2,10},{10... | collective-permute-start | bytes 393224 | tf_op jit(solution)/shard_map/ppermute | solution.py:22
  200.1 31.0 %collective-permute-start.10 = (bf16[4,2,128,256]{3,2,1,0:T(8,128)(2,1)}, bf16[4,2,128,256]{3,2,1,0:T(8,128)(2,1)S(1)}, u32[]{:S(2)}, u32[]{:S(2)}) collective-permute-start(bf16[4,2,128,256]{3,2,1,0:T(8,128)(2,1)} %get-tuple-element.48), channel_id=1, source_target_pairs={{0,8},{8,16},{16,24},{24,0},{1,9},{9,17},{17,25},{25,1},{2,10},{10... | collective-permute-start | bytes 1572872 | tf_op jit(solution)/shard_map/ppermute | solution.py:22
  201.5 30.2 %collective-permute-start.11 = (bf16[4,2,128,256]{3,2,1,0:T(8,128)(2,1)}, bf16[4,2,128,256]{3,2,1,0:T(8,128)(2,1)S(1)}, u32[]{:S(2)}, u32[]{:S(2)}) collective-permute-start(bf16[4,2,128,256]{3,2,1,0:T(8,128)(2,1)} %get-tuple-element.49), channel_id=1, source_target_pairs={{0,24},{8,0},{16,8},{24,16},{1,25},{9,1},{17,9},{25,17},{2,26},{10... | collective-permute-start | bytes 1572872 | tf_op jit(solution)/shard_map/ppermute | solution.py:22
  202.8 28.9 %collective-permute-start.12 = (bf16[4,2,128,256]{3,2,1,0:T(8,128)(2,1)}, bf16[4,2,128,256]{3,2,1,0:T(8,128)(2,1)}, u32[]{:S(2)}, u32[]{:S(2)}) collective-permute-start(bf16[4,2,128,256]{3,2,1,0:T(8,128)(2,1)} %get-tuple-element.50), channel_id=1, source_target_pairs={{0,16},{8,24},{16,0},{24,8},{1,17},{9,25},{17,1},{25,9},{2,18},{10... | collective-permute-start | bytes 1572872 | tf_op jit(solution)/shard_map/ppermute | solution.py:22
  203.7 23.7 %collective-permute-start.32 = (bf16[2,128,256]{2,1,0:T(8,128)(2,1)}, bf16[2,128,256]{2,1,0:T(8,128)(2,1)S(1)}, u32[]{:S(2)}, u32[]{:S(2)}) collective-permute-start(bf16[2,128,256]{2,1,0:T(8,128)(2,1)} %get-tuple-element.99), channel_id=1, source_target_pairs={{0,24},{8,0},{16,8},{24,16},{1,25},{9,1},{17,9},{25,17},{2,26},{10... | collective-permute-start | bytes 393224 | tf_op jit(solution)/shard_map/ppermute | solution.py:22
  205.4 22.9 %collective-permute-start.33 = (bf16[2,128,256]{2,1,0:T(8,128)(2,1)}, bf16[2,128,256]{2,1,0:T(8,128)(2,1)S(1)}, u32[]{:S(2)}, u32[]{:S(2)}) collective-permute-start(bf16[2,128,256]{2,1,0:T(8,128)(2,1)} %get-tuple-element.98), channel_id=1, source_target_pairs={{0,16},{8,24},{16,0},{24,8},{1,17},{9,25},{17,1},{25,9},{2,18},{10... | collective-permute-start | bytes 393224 | tf_op jit(solution)/shard_map/ppermute | solution.py:22
  227.4 13.5 %collective-permute-start.16 = (bf16[4,2,128,256]{3,2,1,0:T(8,128)(2,1)}, bf16[4,2,128,256]{3,2,1,0:T(8,128)(2,1)S(1)}, u32[]{:S(2)}, u32[]{:S(2)}) collective-permute-start(bf16[4,2,128,256]{3,2,1,0:T(8,128)(2,1)} %copy-done.17), channel_id=1, source_target_pairs={{0,2},{2,4},{4,6},{6,0},{1,3},{3,5},{5,7},{7,1},{8,10},{10,12},{12... | collective-permute-start | bytes 1572872 | tf_op jit(solution)/shard_map/ppermute | solution.py:22
  228.3 12.6 %collective-permute-start.17 = (bf16[4,2,128,256]{3,2,1,0:T(8,128)(2,1)}, bf16[4,2,128,256]{3,2,1,0:T(8,128)(2,1)S(1)}, u32[]{:S(2)}, u32[]{:S(2)}) collective-permute-start(bf16[4,2,128,256]{3,2,1,0:T(8,128)(2,1)} %copy-done.16), channel_id=1, source_target_pairs={{0,6},{2,0},{4,2},{6,4},{1,7},{3,1},{5,3},{7,5},{8,14},{10,8},{12,... | collective-permute-start | bytes 1572872 | tf_op jit(solution)/shard_map/ppermute | solution.py:22
  231.2 15.4 %collective-permute-start.18 = (bf16[4,2,128,256]{3,2,1,0:T(8,128)(2,1)S(1)}, bf16[4,2,128,256]{3,2,1,0:T(8,128)(2,1)S(1)}, u32[]{:S(2)}, u32[]{:S(2)}) collective-permute-start(bf16[4,2,128,256]{3,2,1,0:T(8,128)(2,1)S(1)} %get-tuple-element.54), channel_id=1, source_target_pairs={{0,4},{2,6},{4,0},{6,2},{1,5},{3,7},{5,1},{7,3},{8,12},{10,14},{12... | collective-permute-start | bytes 1572872 | tf_op jit(solution)/shard_map/ppermute | solution.py:22
  233.1 16.6 %collective-permute-start.13 = (bf16[2,128,256]{2,1,0:T(8,128)(2,1)S(1)}, bf16[2,128,256]{2,1,0:T(8,128)(2,1)S(1)}, u32[]{:S(2)}, u32[]{:S(2)}) collective-permute-start(bf16[2,128,256]{2,1,0:T(8,128)(2,1)S(1)} %get-tuple-element.88), channel_id=1, source_target_pairs={{0,2},{2,4},{4,6},{6,0},{1,3},{3,5},{5,7},{7,1},{8,10},{10,12},{12... | collective-permute-start | bytes 393224 | tf_op jit(solution)/shard_map/ppermute | solution.py:22
  233.3 17.5 %collective-permute-start.14 = (bf16[2,128,256]{2,1,0:T(8,128)(2,1)S(1)}, bf16[2,128,256]{2,1,0:T(8,128)(2,1)S(1)}, u32[]{:S(2)}, u32[]{:S(2)}) collective-permute-start(bf16[2,128,256]{2,1,0:T(8,128)(2,1)S(1)} %get-tuple-element.90), channel_id=1, source_target_pairs={{0,6},{2,0},{4,2},{6,4},{1,7},{3,1},{5,3},{7,5},{8,14},{10,8},{12,... | collective-permute-start | bytes 393224 | tf_op jit(solution)/shard_map/ppermute | solution.py:22
  240.9 11.5 %collective-permute-start.15 = (bf16[2,128,256]{2,1,0:T(8,128)(2,1)S(1)}, bf16[2,128,256]{2,1,0:T(8,128)(2,1)S(1)}, u32[]{:S(2)}, u32[]{:S(2)}) collective-permute-start(bf16[2,128,256]{2,1,0:T(8,128)(2,1)S(1)} %get-tuple-element.89), channel_id=1, source_target_pairs={{0,4},{2,6},{4,0},{6,2},{1,5},{3,7},{5,1},{7,3},{8,12},{10,14},{12... | collective-permute-start | bytes 393224 | tf_op jit(solution)/shard_map/ppermute | solution.py:22
  271.3 14.1 %collective-permute-start.37 = (f32[3]{0:T(128)S(1)}, f32[3]{0:T(128)S(1)}, u32[]{:S(2)}, u32[]{:S(2)}) collective-permute-start(f32[3]{0:T(128)S(1)} %pad_maximum_fusion.2), channel_id=1, source_target_pairs={{0,1},{1,0},{2,3},{3,2},{4,5},{5,4},{6,7},{7,6},{8,9},{9,8},{10,11... | collective-permute-start | bytes 44 | tf_op jit(solution)/shard_map/ppermute | solution.py:26
  (43 other events, 200.4 us)
Sparse Core Ops, SparseCore 0:
  11.6 107.5 all-gather.2
where the time goes:
time: 322 us; the launch traced here: 318 us
  waiting for transfers between devices  162 us (50%)
  starting transfers between devices  74.1 us (23%)
  Pallas kernels  33 us (10%)
  between operations  21.5 us (7%)
  local copies, waits for them, and re-layouts  16.6 us (5%)
  other arithmetic  10.4 us (3%)
    all_gather x1, waiting for transfers between devices, local(): gathered = lax.all_gather(chunk, ('y', 'z', 'x'), axis=0, tiled=True)  102 us
    ppermute x36, waiting for transfers between devices, shift(): return lax.ppermute(value, axis, [(i, (i + steps) % 4) for i in range(4)])  53 us
    ppermute x36, starting transfers between devices, shift(): return lax.ppermute(value, axis, [(i, (i + steps) % 4) for i in range(4)])  45.5 us
    ppermute x11, starting transfers between devices, swap(): return lax.ppermute(value, 'c', [(0, 1), (1, 0)])  28.5 us
    pallas_call x3, Pallas kernels, local(): call(functools.partial(backward_kernel, layer), [VMEM] * 6 + [ANY], [wide...  11.6 us
    pallas_call x3, Pallas kernels, local(): call(functools.partial(forward_kernel, layer), [VMEM, VMEM, VMEM, ANY], [...  11 us
    unnamed x43, local copies, waits for them, and re-layouts  9.83 us
    ppermute x11, waiting for transfers between devices, swap(): return lax.ppermute(value, 'c', [(0, 1), (1, 0)])  6.99 us
  transfers between devices with their start and end apart: 48, of which 23 were waited for; matrix products, arithmetic and copies ran while one was open for 3% of the time, Pallas kernels for 5%

commit v1 on v0

--- a/solution.py
+++ b/solution.py
@@ -116,14 +116,16 @@
 
 
 def forward_kernel(
-    layer, x_ref, own_ref, got_ref, w_ref, xo_ref, part_ref, buf0, buf1, sems0, sems1
+    layer, x_ref, own_ref, got_ref, w_ref, xo_ref, part_ref, full_ref, buf0, buf1, sems0, sems1
 ):
     ends = fetches(w_ref, layer - 1, 2, buf0, sems0)
     starts = fetches(w_ref, layer, 0, buf1, sems1)
     for i in range(4):
         ends[i].start()
         starts[i].start()
-    mid = middle(own_ref[...] + got_ref[...])
+    full = own_ref[...] + got_ref[...]
+    full_ref[...] = full
+    mid = middle(full)
     act, act_dot = mid[7], mid[8]
     pair = jnp.concatenate([act, act_dot], 0)
     both = jnp.zeros((2 * ROWS, RANK), F32)
@@ -148,11 +150,15 @@
     write_sums(part_ref, both[:ROWS], both[ROWS:] + cross, s1, s2)
 
 
-def seed_kernel(x_ref, own_ref, got_ref, goal_ref, w_ref, cot_ref, part_ref, buf, sems):
+def seed_kernel(
+    x_ref, own_ref, got_ref, goal_ref, w_ref, cot_ref, part_ref, full_ref, buf, sems
+):
     ends = fetches(w_ref, LAYERS - 1, 2, buf, sems)
     for copy in ends:
         copy.start()
-    mid = middle(own_ref[...] + got_ref[...])
+    full = own_ref[...] + got_ref[...]
+    full_ref[...] = full
+    mid = middle(full)
     act, act_dot = mid[7], mid[8]
     pair = jnp.concatenate([act, act_dot], 0)
     both = jnp.zeros((2 * ROWS, RANK), F32)
@@ -178,13 +184,13 @@
     layer,
     x_ref,
     cot_ref,
-    own_ref,
-    got_ref,
+    full_ref,
     e_own_ref,
     e_got_ref,
     w_ref,
     out_ref,
     part_ref,
+    e_full_ref,
     buf0,
     buf1,
     sems0,
@@ -195,9 +201,11 @@
     for i in range(4):
         ends[i].start()
         starts[i].start()
-    mid = middle(own_ref[...] + got_ref[...])
+    mid = middle(full_ref[...])
     u, v, r, c = mid[:4]
-    s, s_dot = inner_cotangents(mid, e_own_ref[...] + e_got_ref[...])
+    e_full = e_own_ref[...] + e_got_ref[...]
+    e_full_ref[...] = e_full
+    s, s_dot = inner_cotangents(mid, e_full)
     pair = jnp.concatenate([s, s_dot], 0)
     sf, sdf = s.astype(F32), s_dot.astype(F32)
     mean = jnp.sum(sf * u, axis=1, keepdims=True) * (1.0 / D)
@@ -229,14 +237,18 @@
 
 
 def hessian_kernel(place_ref, *refs):
-    inputs, downs, ups = refs[:12], refs[12:16], refs[16:20]
+    (x0, cot0, full0, e_own, e_got, x1, cot1, full1, e_full) = refs[:9]
+    downs, ups = refs[9:13], refs[13:17]
+    layers = (
+        (x0, cot0, full0, lambda: e_own[...] + e_got[...]),
+        (x1, cot1, full1, lambda: e_full[...]),
+    )
     me_z, me_x = place_ref[0], place_ref[1]
-    for i in range(2):
-        x_ref, cot_ref, own_ref, got_ref, e_own_ref, e_got_ref = inputs[6 * i : 6 * i + 6]
-        mid = middle(own_ref[...] + got_ref[...])
+    for i, (x_ref, cot_ref, full_ref, e_sum) in enumerate(layers):
+        mid = middle(full_ref[...])
         r, c, act, act_dot = mid[2], mid[3], mid[7], mid[8]
         r3c = r * r * r * c
-        s, s_dot = inner_cotangents(mid, e_own_ref[...] + e_got_ref[...])
+        s, s_dot = inner_cotangents(mid, e_sum())
         pair = jnp.concatenate([s, s_dot], 0)
         acts = jnp.concatenate([act_dot, act], 0)
         for slot_z, far_z in enumerate((0, 1, 3, 2)):
@@ -252,6 +264,48 @@
                 ups[slot_x][slot_z, i] = mm_tn(cot_ref[:, cols], acts).astype(BF16)
 
 
+def ring_kernel(*refs):
+    groups, outs = (refs[4:8], refs[:4]), refs[8:]
+    for slot in range(4):
+        for group, parts in enumerate(groups):
+            total = parts[0][slot].astype(F32)
+            for part in parts[1:]:
+                total += part[slot].astype(F32)
+            outs[slot][2 * group : 2 * group + 2] = total.astype(BF16)
+
+
+def layer_kernel(place_ref, *refs):
+    downs, ups, outs = refs[:4], refs[4:8], refs[8:]
+    for slot, far in enumerate((0, 1, 3, 2)):
+        layer = (place_ref[2] + far) & 3
+        for half, parts in enumerate((downs, ups)):
+            total = parts[0][layer].astype(F32)
+            for part in parts[1:]:
+                total += part[layer].astype(F32)
+            outs[slot][128 * half : 128 * half + 128] = total.astype(BF16)
+
+
+def totals_kernel(b0, b1, b2, b3, gain_ref, vector_ref, share_ref, totals_ref):
+    share = b0[...].astype(F32) + b1[...].astype(F32) + b2[...].astype(F32) + b3[...].astype(F32)
+    share = jnp.concatenate([share[:128] * gain_ref[...], share[128:]], 0)
+    share_ref[...] = share
+    vector = vector_ref[...].astype(F32)
+    row = lax.broadcasted_iota(jnp.int32, (8, 128), 0)
+    totals = jnp.zeros((8, 128), F32)
+    for i, product in enumerate((share * share, vector * share, vector * vector)):
+        total = jnp.sum(jnp.sum(product, axis=0, keepdims=True), axis=1, keepdims=True)
+        totals = jnp.where(row == i, total, totals)
+    totals_ref[...] = totals
+
+
+def output_kernel(share_ref, totals_ref, down_ref, up_ref, quotient_ref):
+    means = totals_ref[...] * (1.0 / (2.0 * LAYERS * D * RANK))
+    scale = 1.0 / jnp.sqrt(means[0:1, 0:1] + EPS)
+    down_ref[...] = (share_ref[:128] * scale).astype(BF16)
+    up_ref[...] = (share_ref[128:] * scale).T.astype(BF16)
+    quotient_ref[...] = means[1:2] / (means[2:3] + EPS) * (1.0 / TOKENS)
+
+
 VMEM = pl.BlockSpec(memory_space=pltpu.VMEM)
 ANY = pl.BlockSpec(memory_space=pl.ANY)
 SMEM = pl.BlockSpec(memory_space=pltpu.SMEM)
@@ -263,34 +317,21 @@
     return jax.ShapeDtypeStruct(dims, dtype)
 
 
-def call(kernel, in_specs, outs, scratch, flops, moved):
+def call(kernel, in_specs, outs, scratch=(), flops=1 << 20, moved=1 << 20):
     return pl.pallas_call(
         kernel,
         in_specs=in_specs,
         out_specs=[VMEM] * len(outs),
         out_shape=outs,
-        scratch_shapes=scratch,
+        scratch_shapes=list(scratch),
         compiler_params=pltpu.CompilerParams(vmem_limit_bytes=40 * 1024 * 1024),
         cost_estimate=pl.CostEstimate(flops=flops, bytes_accessed=moved, transcendentals=0),
     )
 
 
-def direct_scatter(slots, axis):
-    own, ahead, behind, across = slots
-    return (
-        own.astype(F32)
-        + shift(ahead, axis, 1).astype(F32)
-        + shift(behind, axis, -1).astype(F32)
-        + shift(across, axis, 2).astype(F32)
-    )
-
-
-def slots_of(value, axis_name, dim):
-    me = lax.axis_index(axis_name)
-    return [
-        lax.dynamic_index_in_dim(value, (me + step) % 4, dim, keepdims=False)
-        for step in (0, 1, 3, 2)
-    ]
+def received(blocks, axis):
+    own, ahead, behind, across = blocks
+    return [own, shift(ahead, axis, 1), shift(behind, axis, -1), shift(across, axis, 2)]
 
 
 def sum_all(value):
@@ -316,7 +357,7 @@
     h = core_rows(tokens, core)
     goal = core_rows(targets, core)
     x = jnp.concatenate([h, jnp.zeros_like(h)], 0)
-    place = jnp.stack([lax.axis_index("z"), lax.axis_index("x")]).astype(jnp.int32)
+    place = jnp.stack([lax.axis_index("z"), lax.axis_index("x"), lax.axis_index("y")]).astype(jnp.int32)
     wide = shape((2 * ROWS, HALF), BF16)
     sums = shape((ROWS, 640), F32)
     e_sums = shape((ROWS, 512), F32)
@@ -325,79 +366,75 @@
     def exchanged(part):
         return part, swap(part)
 
-    states, sides, cots, e_sides = [x], [], {}, {}
+    states, fulls, cots, e_fulls = [x], [], {}, {}
     (part,) = call(first_kernel, [VMEM, ANY], [sums], [BUF, SEMS], work // 3, 3 << 20)(x, gathered)
-    sides.append(exchanged(part))
     for layer in range(1, LAYERS):
-        x, part = call(
+        x, part, full = call(
             functools.partial(forward_kernel, layer),
             [VMEM, VMEM, VMEM, ANY],
-            [wide, sums],
+            [wide, sums, sums],
             [BUF, BUF, SEMS, SEMS],
             work,
             5 << 20,
-        )(x, *sides[-1], gathered)
+        )(x, part, swap(part), gathered)
         states.append(x)
-        sides.append(exchanged(part))
-    cot, part = call(
+        fulls.append(full)
+    cot, part, full = call(
         seed_kernel,
         [VMEM, VMEM, VMEM, VMEM, ANY],
-        [wide, e_sums],
+        [wide, e_sums, sums],
         [BUF, SEMS],
         work,
         3 << 20,
-    )(x, *sides[-1], goal, gathered)
+    )(x, part, swap(part), goal, gathered)
+    fulls.append(full)
 
     slot = shape((4, 2, 128, RANK), BF16)
-    shares = [None, None]
+    down_parts, up_parts = [], []
     for layer in reversed(range(LAYERS)):
         cots[layer] = cot
-        e_sides[layer] = exchanged(part)
+        e_own, e_got = part, swap(part)
         if layer > 0:
-            cot, part = call(
+            cot, part, e_fulls[layer] = call(
                 functools.partial(backward_kernel, layer),
-                [VMEM] * 6 + [ANY],
-                [wide, e_sums],
+                [VMEM] * 5 + [ANY],
+                [wide, e_sums, e_sums],
                 [BUF, BUF, SEMS, SEMS],
                 work,
                 5 << 20,
-            )(states[layer], cot, *sides[layer], *e_sides[layer], gathered)
+            )(states[layer], cot, fulls[layer], e_own, e_got, gathered)
         if layer in (2, 0):
-            operands = []
-            for one in (layer, layer + 1):
-                operands += [states[one], cots[one], *sides[one], *e_sides[one]]
+            above = layer + 1
             blocks = call(
-                hessian_kernel, [SMEM] + [VMEM] * 12, [slot] * 8, [], 2 * work, 6 << 20
-            )(place, *operands)
-            down = direct_scatter(blocks[:4], "z").astype(BF16)
-            up = direct_scatter(blocks[4:], "x").astype(BF16)
-            down = direct_scatter(list(down), "x").astype(BF16)
-            up = direct_scatter(list(up), "z").astype(BF16)
-            shares[layer // 2] = jnp.concatenate([down, up], 1)
-
-    both = jnp.concatenate([shares[0], shares[1]], 0)
-    share = direct_scatter(slots_of(both, "y", 0), "y")
-    share_down = share[:128] * gain
-    share_up = share[128:].T
-    own_down = down_vector[0].astype(F32)
-    own_up = up_vector[0].astype(F32)
-    totals = jnp.stack(
-        [
-            jnp.sum(share_down * share_down) + jnp.sum(share_up * share_up),
-            jnp.sum(own_down * share_down) + jnp.sum(own_up * share_up),
-            jnp.sum(own_down * own_down) + jnp.sum(own_up * own_up),
-        ]
-    )
+                hessian_kernel, [SMEM] + [VMEM] * 9, [slot] * 8, [], 2 * work, 6 << 20
+            )(
+                place,
+                *(states[layer], cots[layer], fulls[layer], e_own, e_got),
+                *(states[above], cots[above], fulls[above], e_fulls[above]),
+            )
+            down_parts += received(blocks[:4], "z")
+            up_parts += received(blocks[4:], "x")
+
+    four = shape((LAYERS, 128, RANK), BF16)
+    downs = call(ring_kernel, [VMEM] * 8, [four] * 4, moved=5 << 20)(*down_parts)
+    downs = received(downs, "x")
+    ups = call(ring_kernel, [VMEM] * 8, [four] * 4, moved=5 << 20)(*up_parts)
+    ups = received(ups, "z")
+    blocks = call(
+        layer_kernel, [SMEM] + [VMEM] * 8, [shape((256, RANK), BF16)] * 4, moved=2 << 20
+    )(place, *downs, *ups)
+    share, totals = call(
+        totals_kernel,
+        [VMEM] * 6,
+        [shape((256, RANK), F32), shape((8, 128), F32)],
+    )(*received(blocks, "y"), gain, jnp.concatenate([down_vector[0], up_vector[0].T], 0))
     totals = sum_all(totals)
-    total_count = 2.0 * LAYERS * D * RANK
-    square_mean = totals[0] / total_count
-    cross_mean = totals[1] / total_count
-    vector_mean = totals[2] / total_count
-    scale_rms = jnp.sqrt(square_mean + EPS)
-    quotient = cross_mean / (vector_mean + EPS) / TOKENS
-    next_down = (share_down / scale_rms).astype(BF16)[None]
-    next_up = (share_up / scale_rms).astype(BF16)[None]
-    return (next_down, next_up, quotient)
+    next_down, next_up, quotient = call(
+        output_kernel,
+        [VMEM] * 2,
+        [shape((128, RANK), BF16), shape((RANK, 128), BF16), shape((1, 128), F32)],
+    )(share, totals)
+    return (next_down[None], next_up[None], quotient[0, 0])
 
 
 def solution(mesh):

time: 322 us -> 293 us (0.910)
  starting transfers between devices: 74.1 us -> 60.4 us
  other arithmetic: 10.4 us -> 2.68 us
  between operations: 21.5 us -> 14.3 us
  local copies, waits for them, and re-layouts: 16.6 us -> 9.76 us
  waiting for transfers between devices: 162 us -> 167 us
    ppermute x11, starting transfers between devices: 28.5 us -> 13.7 us  [swap(): return lax.ppermute(value, 'c', [(0, 1), (1, 0)])]
    unnamed x43 -> x18, local copies, waits for them, and re-layouts: 9.83 us -> 5.1 us
    convert_element_type x8 -> x0, other arithmetic: 4.45 us -> none  [the longest x2 1.6 us: local(): down = direct_scatter(blocks[:4], 'z').astype(BF16)]
    ppermute x36 -> x30, waiting for transfers between devices: 53 us -> 57.4 us  [shift(): return lax.ppermute(value, axis, [(i, (i + steps) % 4) for i in range(4)])]
    pallas_call x6 -> x11, Pallas kernels: 20.3 us -> 22.5 us  [the longest x3 12.1 us: local(): call(functools.partial(backward_kernel, layer), [VMEM] * 5 + [ANY], [wide...]
    ppermute x36 -> x30, starting transfers between devices: 45.5 us -> 46.6 us  [shift(): return lax.ppermute(value, axis, [(i, (i + steps) % 4) for i in range(4)])]
  transfers between devices with their start and end apart: 48 -> 42, of which waited for: 23 -> 24; matrix products, arithmetic and copies ran while one was open for 3% -> 2% of each run, Pallas kernels for 5% -> 5%
where the time goes in v1:
time: 293 us; the launch traced here: 289 us
  waiting for transfers between devices  167 us (57%)
  starting transfers between devices  60.4 us (21%)
  Pallas kernels  35 us (12%)
  between operations  14.3 us (5%)
  local copies, waits for them, and re-layouts  9.76 us (3%)
    all_gather x1, waiting for transfers between devices, local(): gathered = lax.all_gather(chunk, ('y', 'z', 'x'), axis=0, tiled=True)  102 us
    ppermute x30, waiting for transfers between devices, shift(): return lax.ppermute(value, axis, [(i, (i + steps) % 4) for i in range(4)])  57.4 us
    ppermute x30, starting transfers between devices, shift(): return lax.ppermute(value, axis, [(i, (i + steps) % 4) for i in range(4)])  46.6 us
    ppermute x11, starting transfers between devices, swap(): return lax.ppermute(value, 'c', [(0, 1), (1, 0)])  13.7 us
    pallas_call x3, Pallas kernels, local(): call(functools.partial(backward_kernel, layer), [VMEM] * 5 + [ANY], [wide...  12.1 us
    pallas_call x3, Pallas kernels, local(): call(functools.partial(forward_kernel, layer), [VMEM, VMEM, VMEM, ANY], [...  10.8 us
    ppermute x11, waiting for transfers between devices, swap(): return lax.ppermute(value, 'c', [(0, 1), (1, 0)])  7 us
  transfers between devices with their start and end apart: 42, of which 24 were waited for; matrix products, arithmetic and copies ran while one was open for 2% of the time, Pallas kernels for 5%

profile of v1, /device:TPU:1, one launch (start us, length us, event | category | flops | bytes accessed | tf_op | source)
XLA Modules:
  0.0 288.9 jit_solution(9516249194223980626)
XLA Ops:
  17.0 102.3 %all-gather.3.cloned.1.call-done = bf16[256,128,256]{2,1,0:T(8,128)(2,1)} async-done(((bf16[4,128,256]{2,1,0:T(8,128)(2,1)}), bf16[256,128,256]{2,1,0:T(8,128)(2,1)}) %all-gather.3.cloned.1.call-update) | async-done | bytes 16777232 | tf_op jit(solution)/shard_map/all_gather | solution.py:355
  122.8 3.6 %shard_map.95 = (bf16[128,2048]{1,0:T(8,128)(2,1)S(1)}, f32[64,640]{1,0:T(8,128)S(1)}, f32[64,640]{1,0:T(8,128)S(1)}) custom-call(bf16[128,2048]{1,0:T(8,128)(2,1)S(1)} %maximum_maximum_fusion.x_ref.refs_0_, f32[64,640]{1,0:T(8,128)S(1)} %shard_map.94.own_ref, f32[64,640]{1,0:T(8,128)S(1)} %collective-permute-done.1.got_ref, ...), custom_call_target="tpu_custom_call" | custom-call | flops 402653184 | bytes 5242880 | tf_op jit(solution)/shard_map/pallas_call | solution.py:372
  128.9 3.6 %shard_map.96 = (bf16[128,2048]{1,0:T(8,128)(2,1)S(1)}, f32[64,640]{1,0:T(8,128)S(1)}, f32[64,640]{1,0:T(8,128)S(1)}) custom-call(bf16[128,2048]{1,0:T(8,128)(2,1)S(1)} %get-tuple-element.56.x_ref.refs_5_, f32[64,640]{1,0:T(8,128)S(1)} %get-tuple-element.57.own_ref, f32[64,640]{1,0:T(8,128)S(1)} %collective-permute-done.2.got_ref, ...), custom_call_target="tpu_custom_call" | custom-call | flops 402653184 | bytes 5242880 | tf_op jit(solution)/shard_map/pallas_call | solution.py:372
  133.9 3.6 %shard_map.97 = (bf16[128,2048]{1,0:T(8,128)(2,1)S(1)}, f32[64,640]{1,0:T(8,128)S(1)}, f32[64,640]{1,0:T(8,128)S(1)}) custom-call(bf16[128,2048]{1,0:T(8,128)(2,1)S(1)} %get-tuple-element.58.x_ref.refs_0_, f32[64,640]{1,0:T(8,128)S(1)} %get-tuple-element.59.own_ref, f32[64,640]{1,0:T(8,128)S(1)} %collective-permute-done.3.got_ref, ...), custom_call_target="tpu_custom_call" | custom-call | flops 402653184 | bytes 5242880 | tf_op jit(solution)/shard_map/pallas_call | solution.py:372
  139.0 2.9 %shard_map.98 = (bf16[128,2048]{1,0:T(8,128)(2,1)S(1)}, f32[64,512]{1,0:T(8,128)S(1)}, f32[64,640]{1,0:T(8,128)S(1)}) custom-call(bf16[128,2048]{1,0:T(8,128)(2,1)S(1)} %get-tuple-element.60.x_ref.refs_5_, f32[64,640]{1,0:T(8,128)S(1)} %get-tuple-element.61.own_ref, f32[64,640]{1,0:T(8,128)S(1)} %collective-permute-done.4.got_ref, ...), custom_call_target="tpu_custom_call" | custom-call | flops 402653184 | bytes 3145728 | tf_op jit(solution)/shard_map/pallas_call | solution.py:382
  143.6 4.0 %shard_map.99 = (bf16[128,2048]{1,0:T(8,128)(2,1)S(1)}, f32[64,512]{1,0:T(8,128)}, f32[64,512]{1,0:T(8,128)S(1)}) custom-call(bf16[128,2048]{1,0:T(8,128)(2,1)S(1)} %get-tuple-element.60.x_ref.refs_5_, bf16[128,2048]{1,0:T(8,128)(2,1)S(1)} %get-tuple-element.62.cot_ref.refs_6_, f32[64,640]{1,0:T(8,128)S(1)} %get-tuple-element.63.full_ref.refs_7_, ...), custom_call_target="tpu_custom_call" | custom-call | flops 402653184 | bytes 5242880 | tf_op jit(solution)/shard_map/pallas_call | solution.py:398
  157.7 4.7 %shard_map.101 = (bf16[128,2048]{1,0:T(8,128)(2,1)S(1)}, f32[64,512]{1,0:T(8,128)S(1)}, f32[64,512]{1,0:T(8,128)}) custom-call(bf16[128,2048]{1,0:T(8,128)(2,1)S(1)} %get-tuple-element.58.x_ref.refs_0_, bf16[128,2048]{1,0:T(8,128)(2,1)S(1)} %get-tuple-element.65.refs_1_.cot_ref, f32[64,640]{1,0:T(8,128)S(1)} %get-tuple-element.66.refs_2_.full_ref, ...), custom_call_target="tpu_custom_call" | custom-call | flops 402653184 | bytes 5242880 | tf_op jit(solution)/shard_map/pallas_call | solution.py:398
  165.0 3.4 %shard_map.102 = (bf16[128,2048]{1,0:T(8,128)(2,1)S(1)}, f32[64,512]{1,0:T(8,128)S(1)}, f32[64,512]{1,0:T(8,128)S(1)}) custom-call(bf16[128,2048]{1,0:T(8,128)(2,1)S(1)} %get-tuple-element.56.x_ref.refs_5_, bf16[128,2048]{1,0:T(8,128)(2,1)S(1)} %get-tuple-element.73.cot_ref.refs_6_, f32[64,640]{1,0:T(8,128)S(1)} %get-tuple-element.74.full_ref.refs_7_, ...), custom_call_target="tpu_custom_call" | custom-call | flops 402653184 | bytes 5242880 | tf_op jit(solution)/shard_map/pallas_call | solution.py:398
  176.0 5.6 %collective-permute-done.21.refs_3_ = bf16[4,2,128,256]{3,2,1,0:T(8,128)(2,1)S(1)} collective-permute-done((bf16[4,2,128,256]{3,2,1,0:T(8,128)(2,1)S(1)}, bf16[4,2,128,256]{3,2,1,0:T(8,128)(2,1)S(1)}, u32[]{:S(2)}, u32[]{:S(2)}) %collective-permute-start.21) | collective-permute-done | bytes 524320 | tf_op jit(solution)/shard_map/ppermute | solution.py:22
  185.6 8.6 %collective-permute-done.22.refs_5_ = bf16[4,2,128,256]{3,2,1,0:T(8,128)(2,1)S(1)} collective-permute-done((bf16[4,2,128,256]{3,2,1,0:T(8,128)(2,1)S(1)}, bf16[4,2,128,256]{3,2,1,0:T(8,128)(2,1)S(1)}, u32[]{:S(2)}, u32[]{:S(2)}) %collective-permute-start.22) | collective-permute-done | bytes 524320 | tf_op jit(solution)/shard_map/ppermute | solution.py:22
  196.9 7.2 %collective-permute-done.24.refs_7_ = bf16[4,2,128,256]{3,2,1,0:T(8,128)(2,1)S(1)} collective-permute-done((bf16[4,2,128,256]{3,2,1,0:T(8,128)(2,1)S(1)}, bf16[4,2,128,256]{3,2,1,0:T(8,128)(2,1)S(1)}, u32[]{:S(2)}, u32[]{:S(2)}) %collective-permute-start.24) | collective-permute-done | bytes 524320 | tf_op jit(solution)/shard_map/ppermute | solution.py:22
  209.5 10.5 %collective-permute-done.15.refs_7_ = bf16[4,2,128,256]{3,2,1,0:T(8,128)(2,1)S(1)} collective-permute-done((bf16[4,2,128,256]{3,2,1,0:T(8,128)(2,1)S(1)}, bf16[4,2,128,256]{3,2,1,0:T(8,128)(2,1)S(1)}, u32[]{:S(2)}, u32[]{:S(2)}) %collective-permute-start.15) | collective-permute-done | bytes 524320 | tf_op jit(solution)/shard_map/ppermute | solution.py:22
  220.6 2.7 collective-permute-start.17
  223.3 4.0 %collective-permute-done.25.refs_5_ = bf16[4,128,256]{2,1,0:T(8,128)(2,1)S(1)} collective-permute-done((bf16[4,128,256]{2,1,0:T(8,128)(2,1)S(1)}, bf16[4,128,256]{2,1,0:T(8,128)(2,1)S(1)}, u32[]{:S(2)}, u32[]{:S(2)}) %collective-permute-start.25) | collective-permute-done | bytes 262176 | tf_op jit(solution)/shard_map/ppermute | solution.py:22
  227.8 3.4 %collective-permute-done.27.refs_7_ = bf16[4,128,256]{2,1,0:T(8,128)(2,1)S(1)} collective-permute-done((bf16[4,128,256]{2,1,0:T(8,128)(2,1)S(1)}, bf16[4,128,256]{2,1,0:T(8,128)(2,1)S(1)}, u32[]{:S(2)}, u32[]{:S(2)}) %collective-permute-start.27) | collective-permute-done | bytes 262176 | tf_op jit(solution)/shard_map/ppermute | solution.py:22
  231.3 2.7 collective-permute-done.18.refs_3_
  234.8 9.0 %collective-permute-start.28 = (bf16[256,256]{1,0:T(8,128)(2,1)S(1)}, bf16[256,256]{1,0:T(8,128)(2,1)S(1)}, u32[]{:S(2)}, u32[]{:S(2)}) collective-permute-start(bf16[256,256]{1,0:T(8,128)(2,1)S(1)} %get-tuple-element.101), channel_id=1, source_target_pairs={{0,32},{32,64},{64,96},{96,0},{1,33},{33,65},{65,97},{97,1},{2,34}... | collective-permute-start | bytes 393224 | tf_op jit(solution)/shard_map/ppermute | solution.py:22
  247.6 2.8 collective-permute-done.30.b3
  250.6 7.5 %collective-permute-start.31 = (f32[8,128]{1,0:T(8,128)S(1)}, f32[8,128]{1,0:T(8,128)S(1)}, u32[]{:S(2)}, u32[]{:S(2)}) collective-permute-start(f32[8,128]{1,0:T(8,128)S(1)} %get-tuple-element.105), channel_id=1, source_target_pairs={{0,1},{1,0},{2,3},{3,2},{4,5},{5,4},{6,7},{7,6},{8,9},{9,8},{10,11... | collective-permute-start | bytes 12296 | tf_op jit(solution)/shard_map/ppermute | solution.py:26
  259.0 2.7 collective-permute-start.33
  262.6 3.0 %collective-permute-done.34 = f32[8,128]{1,0:T(8,128)S(1)} collective-permute-done((f32[8,128]{1,0:T(8,128)S(1)}, f32[8,128]{1,0:T(8,128)S(1)}, u32[]{:S(2)}, u32[]{:S(2)}) %collective-permute-start.34) | collective-permute-done | bytes 4128 | tf_op jit(solution)/shard_map/ppermute | solution.py:22
  265.6 5.0 %collective-permute-start.36 = (f32[8,128]{1,0:T(8,128)S(1)}, f32[8,128]{1,0:T(8,128)S(1)}, u32[]{:S(2)}, u32[]{:S(2)}) collective-permute-start(f32[8,128]{1,0:T(8,128)S(1)} %add_add_fusion.2), channel_id=1, source_target_pairs={{0,24},{8,0},{16,8},{24,16},{1,25},{9,1},{17,9},{25,17},{2,26},{10... | collective-permute-start | bytes 12296 | tf_op jit(solution)/shard_map/ppermute | solution.py:22
  271.7 2.8 collective-permute-done.37
  278.2 3.0 %collective-permute-done.40 = f32[8,128]{1,0:T(8,128)S(1)} collective-permute-done((f32[8,128]{1,0:T(8,128)S(1)}, f32[8,128]{1,0:T(8,128)S(1)}, u32[]{:S(2)}, u32[]{:S(2)}) %collective-permute-start.40) | collective-permute-done | bytes 4128 | tf_op jit(solution)/shard_map/ppermute | solution.py:22
  (115 shorter events, 65.9 us)
Async XLA Ops:
  7.2 112.1 %all-gather.3.cloned.1.call-start = ((), (), s32[]{:S(2)}) async-start(), calls=%async_computation | async-start | bytes 17039360 | tf_op jit(solution)/shard_map/all_gather | solution.py:355
  155.0 18.4 %collective-permute-start.19 = (bf16[4,2,128,256]{3,2,1,0:T(8,128)(2,1)S(1)}, bf16[4,2,128,256]{3,2,1,0:T(8,128)(2,1)S(1)}, u32[]{:S(2)}, u32[]{:S(2)}) collective-permute-start(bf16[4,2,128,256]{3,2,1,0:T(8,128)(2,1)S(1)} %get-tuple-element.89), channel_id=1, source_target_pairs={{0,2},{2,4},{4,6},{6,0},{1,3},{3,5},{5,7},{7,1},{8,10},{10,12},{12... | collective-permute-start | bytes 1572872 | tf_op jit(solution)/shard_map/ppermute | solution.py:22
  156.2 19.5 %collective-permute-start.20 = (bf16[4,2,128,256]{3,2,1,0:T(8,128)(2,1)S(1)}, bf16[4,2,128,256]{3,2,1,0:T(8,128)(2,1)S(1)}, u32[]{:S(2)}, u32[]{:S(2)}) collective-permute-start(bf16[4,2,128,256]{3,2,1,0:T(8,128)(2,1)S(1)} %get-tuple-element.90), channel_id=1, source_target_pairs={{0,6},{2,0},{4,2},{6,4},{1,7},{3,1},{5,3},{7,5},{8,14},{10,8},{12,... | collective-permute-start | bytes 1572872 | tf_op jit(solution)/shard_map/ppermute | solution.py:22
  163.4 18.2 %collective-permute-start.21 = (bf16[4,2,128,256]{3,2,1,0:T(8,128)(2,1)S(1)}, bf16[4,2,128,256]{3,2,1,0:T(8,128)(2,1)S(1)}, u32[]{:S(2)}, u32[]{:S(2)}) collective-permute-start(bf16[4,2,128,256]{3,2,1,0:T(8,128)(2,1)S(1)} %get-tuple-element.91), channel_id=1, source_target_pairs={{0,4},{2,6},{4,0},{6,2},{1,5},{3,7},{5,1},{7,3},{8,12},{10,14},{12... | collective-permute-start | bytes 1572872 | tf_op jit(solution)/shard_map/ppermute | solution.py:22
  168.8 14.9 %collective-permute-start.10 = (bf16[4,2,128,256]{3,2,1,0:T(8,128)(2,1)S(1)}, bf16[4,2,128,256]{3,2,1,0:T(8,128)(2,1)S(1)}, u32[]{:S(2)}, u32[]{:S(2)}) collective-permute-start(bf16[4,2,128,256]{3,2,1,0:T(8,128)(2,1)S(1)} %get-tuple-element.72), channel_id=1, source_target_pairs={{0,16},{8,24},{16,0},{24,8},{1,17},{9,25},{17,1},{25,9},{2,18},{10... | collective-permute-start | bytes 1572872 | tf_op jit(solution)/shard_map/ppermute | solution.py:22
  173.0 21.2 %collective-permute-start.22 = (bf16[4,2,128,256]{3,2,1,0:T(8,128)(2,1)S(1)}, bf16[4,2,128,256]{3,2,1,0:T(8,128)(2,1)S(1)}, u32[]{:S(2)}, u32[]{:S(2)}) collective-permute-start(bf16[4,2,128,256]{3,2,1,0:T(8,128)(2,1)S(1)} %get-tuple-element.93), channel_id=1, source_target_pairs={{0,2},{2,4},{4,6},{6,0},{1,3},{3,5},{5,7},{7,1},{8,10},{10,12},{12... | collective-permute-start | bytes 1572872 | tf_op jit(solution)/shard_map/ppermute | solution.py:22
  173.4 21.4 %collective-permute-start.23 = (bf16[4,2,128,256]{3,2,1,0:T(8,128)(2,1)S(1)}, bf16[4,2,128,256]{3,2,1,0:T(8,128)(2,1)S(1)}, u32[]{:S(2)}, u32[]{:S(2)}) collective-permute-start(bf16[4,2,128,256]{3,2,1,0:T(8,128)(2,1)S(1)} %get-tuple-element.94), channel_id=1, source_target_pairs={{0,6},{2,0},{4,2},{6,4},{1,7},{3,1},{5,3},{7,5},{8,14},{10,8},{12,... | collective-permute-start | bytes 1572872 | tf_op jit(solution)/shard_map/ppermute | solution.py:22
  175.7 28.4 %collective-permute-start.24 = (bf16[4,2,128,256]{3,2,1,0:T(8,128)(2,1)S(1)}, bf16[4,2,128,256]{3,2,1,0:T(8,128)(2,1)S(1)}, u32[]{:S(2)}, u32[]{:S(2)}) collective-permute-start(bf16[4,2,128,256]{3,2,1,0:T(8,128)(2,1)S(1)} %get-tuple-element.95), channel_id=1, source_target_pairs={{0,4},{2,6},{4,0},{6,2},{1,5},{3,7},{5,1},{7,3},{8,12},{10,14},{12... | collective-permute-start | bytes 1572872 | tf_op jit(solution)/shard_map/ppermute | solution.py:22
  181.6 25.1 %collective-permute-start.8 = (bf16[4,2,128,256]{3,2,1,0:T(8,128)(2,1)S(1)}, bf16[4,2,128,256]{3,2,1,0:T(8,128)(2,1)S(1)}, u32[]{:S(2)}, u32[]{:S(2)}) collective-permute-start(bf16[4,2,128,256]{3,2,1,0:T(8,128)(2,1)S(1)} %get-tuple-element.70), channel_id=1, source_target_pairs={{0,8},{8,16},{16,24},{24,0},{1,9},{9,17},{17,25},{25,1},{2,10},{10... | collective-permute-start | bytes 1572872 | tf_op jit(solution)/shard_map/ppermute | solution.py:22
  183.7 23.5 %collective-permute-start.9 = (bf16[4,2,128,256]{3,2,1,0:T(8,128)(2,1)S(1)}, bf16[4,2,128,256]{3,2,1,0:T(8,128)(2,1)S(1)}, u32[]{:S(2)}, u32[]{:S(2)}) collective-permute-start(bf16[4,2,128,256]{3,2,1,0:T(8,128)(2,1)S(1)} %get-tuple-element.71), channel_id=1, source_target_pairs={{0,24},{8,0},{16,8},{24,16},{1,25},{9,1},{17,9},{25,17},{2,26},{10... | collective-permute-start | bytes 1572872 | tf_op jit(solution)/shard_map/ppermute | solution.py:22
  194.2 15.3 %collective-permute-start.13 = (bf16[4,2,128,256]{3,2,1,0:T(8,128)(2,1)S(1)}, bf16[4,2,128,256]{3,2,1,0:T(8,128)(2,1)S(1)}, u32[]{:S(2)}, u32[]{:S(2)}) collective-permute-start(bf16[4,2,128,256]{3,2,1,0:T(8,128)(2,1)S(1)} %get-tuple-element.81), channel_id=1, source_target_pairs={{0,8},{8,16},{16,24},{24,0},{1,9},{9,17},{17,25},{25,1},{2,10},{10... | collective-permute-start | bytes 1572872 | tf_op jit(solution)/shard_map/ppermute | solution.py:22
  194.7 14.8 %collective-permute-start.14 = (bf16[4,2,128,256]{3,2,1,0:T(8,128)(2,1)S(1)}, bf16[4,2,128,256]{3,2,1,0:T(8,128)(2,1)S(1)}, u32[]{:S(2)}, u32[]{:S(2)}) collective-permute-start(bf16[4,2,128,256]{3,2,1,0:T(8,128)(2,1)S(1)} %get-tuple-element.82), channel_id=1, source_target_pairs={{0,24},{8,0},{16,8},{24,16},{1,25},{9,1},{17,9},{25,17},{2,26},{10... | collective-permute-start | bytes 1572872 | tf_op jit(solution)/shard_map/ppermute | solution.py:22
  204.1 15.9 %collective-permute-start.15 = (bf16[4,2,128,256]{3,2,1,0:T(8,128)(2,1)S(1)}, bf16[4,2,128,256]{3,2,1,0:T(8,128)(2,1)S(1)}, u32[]{:S(2)}, u32[]{:S(2)}) collective-permute-start(bf16[4,2,128,256]{3,2,1,0:T(8,128)(2,1)S(1)} %get-tuple-element.83), channel_id=1, source_target_pairs={{0,16},{8,24},{16,0},{24,8},{1,17},{9,25},{17,1},{25,9},{2,18},{10... | collective-permute-start | bytes 1572872 | tf_op jit(solution)/shard_map/ppermute | solution.py:22
  206.7 20.5 %collective-permute-start.25 = (bf16[4,128,256]{2,1,0:T(8,128)(2,1)S(1)}, bf16[4,128,256]{2,1,0:T(8,128)(2,1)S(1)}, u32[]{:S(2)}, u32[]{:S(2)}) collective-permute-start(bf16[4,128,256]{2,1,0:T(8,128)(2,1)S(1)} %get-tuple-element.97), channel_id=1, source_target_pairs={{0,8},{8,16},{16,24},{24,0},{1,9},{9,17},{17,25},{25,1},{2,10},{10... | collective-permute-start | bytes 786440 | tf_op jit(solution)/shard_map/ppermute | solution.py:22
  207.2 20.6 %collective-permute-start.26 = (bf16[4,128,256]{2,1,0:T(8,128)(2,1)S(1)}, bf16[4,128,256]{2,1,0:T(8,128)(2,1)S(1)}, u32[]{:S(2)}, u32[]{:S(2)}) collective-permute-start(bf16[4,128,256]{2,1,0:T(8,128)(2,1)S(1)} %get-tuple-element.98), channel_id=1, source_target_pairs={{0,24},{8,0},{16,8},{24,16},{1,25},{9,1},{17,9},{25,17},{2,26},{10... | collective-permute-start | bytes 786440 | tf_op jit(solution)/shard_map/ppermute | solution.py:22
  209.5 21.8 %collective-permute-start.27 = (bf16[4,128,256]{2,1,0:T(8,128)(2,1)S(1)}, bf16[4,128,256]{2,1,0:T(8,128)(2,1)S(1)}, u32[]{:S(2)}, u32[]{:S(2)}) collective-permute-start(bf16[4,128,256]{2,1,0:T(8,128)(2,1)S(1)} %get-tuple-element.99), channel_id=1, source_target_pairs={{0,16},{8,24},{16,0},{24,8},{1,17},{9,25},{17,1},{25,9},{2,18},{10... | collective-permute-start | bytes 786440 | tf_op jit(solution)/shard_map/ppermute | solution.py:22
  220.5 10.7 %collective-permute-start.16 = (bf16[4,128,256]{2,1,0:T(8,128)(2,1)S(1)}, bf16[4,128,256]{2,1,0:T(8,128)(2,1)S(1)}, u32[]{:S(2)}, u32[]{:S(2)}) collective-permute-start(bf16[4,128,256]{2,1,0:T(8,128)(2,1)S(1)} %get-tuple-element.85), channel_id=1, source_target_pairs={{0,2},{2,4},{4,6},{6,0},{1,3},{3,5},{5,7},{7,1},{8,10},{10,12},{12... | collective-permute-start | bytes 786440 | tf_op jit(solution)/shard_map/ppermute | solution.py:22
  220.6 10.6 %collective-permute-start.17 = (bf16[4,128,256]{2,1,0:T(8,128)(2,1)S(1)}, bf16[4,128,256]{2,1,0:T(8,128)(2,1)S(1)}, u32[]{:S(2)}, u32[]{:S(2)}) collective-permute-start(bf16[4,128,256]{2,1,0:T(8,128)(2,1)S(1)} %get-tuple-element.86), channel_id=1, source_target_pairs={{0,6},{2,0},{4,2},{6,4},{1,7},{3,1},{5,3},{7,5},{8,14},{10,8},{12,... | collective-permute-start | bytes 786440 | tf_op jit(solution)/shard_map/ppermute | solution.py:22
  227.3 6.7 %collective-permute-start.18 = (bf16[4,128,256]{2,1,0:T(8,128)(2,1)S(1)}, bf16[4,128,256]{2,1,0:T(8,128)(2,1)S(1)}, u32[]{:S(2)}, u32[]{:S(2)}) collective-permute-start(bf16[4,128,256]{2,1,0:T(8,128)(2,1)S(1)} %get-tuple-element.87), channel_id=1, source_target_pairs={{0,4},{2,6},{4,0},{6,2},{1,5},{3,7},{5,1},{7,3},{8,12},{10,14},{12... | collective-permute-start | bytes 786440 | tf_op jit(solution)/shard_map/ppermute | solution.py:22
  234.8 12.6 %collective-permute-start.28 = (bf16[256,256]{1,0:T(8,128)(2,1)S(1)}, bf16[256,256]{1,0:T(8,128)(2,1)S(1)}, u32[]{:S(2)}, u32[]{:S(2)}) collective-permute-start(bf16[256,256]{1,0:T(8,128)(2,1)S(1)} %get-tuple-element.101), channel_id=1, source_target_pairs={{0,32},{32,64},{64,96},{96,0},{1,33},{33,65},{65,97},{97,1},{2,34}... | collective-permute-start | bytes 393224 | tf_op jit(solution)/shard_map/ppermute | solution.py:22
  245.1 5.3 %collective-permute-start.30 = (bf16[256,256]{1,0:T(8,128)(2,1)S(1)}, bf16[256,256]{1,0:T(8,128)(2,1)S(1)}, u32[]{:S(2)}, u32[]{:S(2)}) collective-permute-start(bf16[256,256]{1,0:T(8,128)(2,1)S(1)} %get-tuple-element.103), channel_id=1, source_target_pairs={{0,64},{32,96},{64,0},{96,32},{1,65},{33,97},{65,1},{97,33},{2,66}... | collective-permute-start | bytes 393224 | tf_op jit(solution)/shard_map/ppermute | solution.py:22
  250.6 8.3 %collective-permute-start.31 = (f32[8,128]{1,0:T(8,128)S(1)}, f32[8,128]{1,0:T(8,128)S(1)}, u32[]{:S(2)}, u32[]{:S(2)}) collective-permute-start(f32[8,128]{1,0:T(8,128)S(1)} %get-tuple-element.105), channel_id=1, source_target_pairs={{0,1},{1,0},{2,3},{3,2},{4,5},{5,4},{6,7},{7,6},{8,9},{9,8},{10,11... | collective-permute-start | bytes 12296 | tf_op jit(solution)/shard_map/ppermute | solution.py:26
  265.6 6.1 %collective-permute-start.35 = (f32[8,128]{1,0:T(8,128)S(1)}, f32[8,128]{1,0:T(8,128)S(1)}, u32[]{:S(2)}, u32[]{:S(2)}) collective-permute-start(f32[8,128]{1,0:T(8,128)S(1)} %add_add_fusion.2), channel_id=1, source_target_pairs={{0,8},{8,16},{16,24},{24,0},{1,9},{9,17},{17,25},{25,1},{2,10},{10... | collective-permute-start | bytes 12296 | tf_op jit(solution)/shard_map/ppermute | solution.py:22
  265.6 6.1 %collective-permute-start.36 = (f32[8,128]{1,0:T(8,128)S(1)}, f32[8,128]{1,0:T(8,128)S(1)}, u32[]{:S(2)}, u32[]{:S(2)}) collective-permute-start(f32[8,128]{1,0:T(8,128)S(1)} %add_add_fusion.2), channel_id=1, source_target_pairs={{0,24},{8,0},{16,8},{24,16},{1,25},{9,1},{17,9},{25,17},{2,26},{10... | collective-permute-start | bytes 12296 | tf_op jit(solution)/shard_map/ppermute | solution.py:22
  (25 other events, 157.0 us)
Sparse Core Ops, SparseCore 0:
  11.6 107.5 all-gather.2

commit v2 on v1

--- a/solution.py
+++ b/solution.py
@@ -238,7 +238,7 @@
 
 def hessian_kernel(place_ref, *refs):
     (x0, cot0, full0, e_own, e_got, x1, cot1, full1, e_full) = refs[:9]
-    downs, ups = refs[9:13], refs[13:17]
+    outs = refs[9:13] + refs[13:14], refs[14:18] + refs[18:19]
     layers = (
         (x0, cot0, full0, lambda: e_own[...] + e_got[...]),
         (x1, cot1, full1, lambda: e_full[...]),
@@ -260,12 +260,30 @@
                 normed = jnp.concatenate(
                     [(r * t - r3c * h).astype(BF16), (r * h).astype(BF16)], 0
                 )
-                downs[slot_z][slot_x, i] = mm_tn(normed, pair).astype(BF16)
-                ups[slot_x][slot_z, i] = mm_tn(cot_ref[:, cols], acts).astype(BF16)
+                down = mm_tn(normed, pair).astype(BF16)
+                up = mm_tn(cot_ref[:, cols], acts).astype(BF16)
+                for refs_, slot, inner, value in (
+                    (outs[0], slot_z, slot_x, down),
+                    (outs[1], slot_x, slot_z, up),
+                ):
+                    if slot < 3:
+                        refs_[slot][inner, i] = value
+                    else:
+                        refs_[3 + inner // 2][inner % 2, i] = value
+
+
+def step_kernel(*refs):
+    for i in range(2):
+        ahead, behind, first, second = refs[4 * i : 4 * i + 4]
+        ahead_out, behind_out = refs[8 + 2 * i : 10 + 2 * i]
+        ahead_out[:2] = (ahead[:2].astype(F32) + first[...].astype(F32)).astype(BF16)
+        ahead_out[2:] = ahead[2:]
+        behind_out[:2] = behind[:2]
+        behind_out[2:] = (behind[2:].astype(F32) + second[...].astype(F32)).astype(BF16)
 
 
 def ring_kernel(*refs):
-    groups, outs = (refs[4:8], refs[:4]), refs[8:]
+    groups, outs = (refs[3:6], refs[:3]), refs[6:]
     for slot in range(4):
         for group, parts in enumerate(groups):
             total = parts[0][slot].astype(F32)
@@ -290,20 +308,22 @@
     share = jnp.concatenate([share[:128] * gain_ref[...], share[128:]], 0)
     share_ref[...] = share
     vector = vector_ref[...].astype(F32)
-    row = lax.broadcasted_iota(jnp.int32, (8, 128), 0)
-    totals = jnp.zeros((8, 128), F32)
+    lane = lax.broadcasted_iota(jnp.int32, (1, 128), 1)
+    totals = jnp.zeros((1, 128), F32)
     for i, product in enumerate((share * share, vector * share, vector * vector)):
         total = jnp.sum(jnp.sum(product, axis=0, keepdims=True), axis=1, keepdims=True)
-        totals = jnp.where(row == i, total, totals)
+        totals = jnp.where(lane == i, total, totals)
     totals_ref[...] = totals
 
 
 def output_kernel(share_ref, totals_ref, down_ref, up_ref, quotient_ref):
-    means = totals_ref[...] * (1.0 / (2.0 * LAYERS * D * RANK))
-    scale = 1.0 / jnp.sqrt(means[0:1, 0:1] + EPS)
+    totals = jnp.sum(totals_ref[...], axis=0, keepdims=True)
+    means = totals * (1.0 / (2.0 * LAYERS * D * RANK))
+    scale = 1.0 / jnp.sqrt(means[:, 0:1] + EPS)
     down_ref[...] = (share_ref[:128] * scale).astype(BF16)
     up_ref[...] = (share_ref[128:] * scale).T.astype(BF16)
-    quotient_ref[...] = means[1:2] / (means[2:3] + EPS) * (1.0 / TOKENS)
+    quotient = means[:, 1:2] / (means[:, 2:3] + EPS) * (1.0 / TOKENS)
+    quotient_ref[...] = jnp.broadcast_to(quotient, (1, 128))
 
 
 VMEM = pl.BlockSpec(memory_space=pltpu.VMEM)
@@ -332,13 +352,6 @@
 def received(blocks, axis):
     own, ahead, behind, across = blocks
     return [own, shift(ahead, axis, 1), shift(behind, axis, -1), shift(across, axis, 2)]
-
-
-def sum_all(value):
-    value = value + swap(value)
-    for axis in ("x", "z", "y"):
-        value = value + shift(value, axis, 1) + shift(value, axis, -1) + shift(value, axis, 2)
-    return value
 
 
 def local(tokens, targets, norm_gain, down_weight, up_weight, down_vector, up_vector):
@@ -390,35 +403,73 @@
     fulls.append(full)
 
     slot = shape((4, 2, 128, RANK), BF16)
+    cut = shape((2, 2, 128, RANK), BF16)
     down_parts, up_parts = [], []
-    for layer in reversed(range(LAYERS)):
-        cots[layer] = cot
-        e_own, e_got = part, swap(part)
-        if layer > 0:
-            cot, part, e_fulls[layer] = call(
-                functools.partial(backward_kernel, layer),
-                [VMEM] * 5 + [ANY],
-                [wide, e_sums, e_sums],
-                [BUF, BUF, SEMS, SEMS],
-                work,
-                5 << 20,
-            )(states[layer], cot, fulls[layer], e_own, e_got, gathered)
-        if layer in (2, 0):
-            above = layer + 1
-            blocks = call(
-                hessian_kernel, [SMEM] + [VMEM] * 9, [slot] * 8, [], 2 * work, 6 << 20
-            )(
-                place,
-                *(states[layer], cots[layer], fulls[layer], e_own, e_got),
-                *(states[above], cots[above], fulls[above], e_fulls[above]),
-            )
-            down_parts += received(blocks[:4], "z")
-            up_parts += received(blocks[4:], "x")
+    def backward(layer, cot, e_own, e_got):
+        return call(
+            functools.partial(backward_kernel, layer),
+            [VMEM] * 5 + [ANY],
+            [wide, e_sums, e_sums],
+            [BUF, BUF, SEMS, SEMS],
+            work,
+            5 << 20,
+        )(states[layer], cot, fulls[layer], e_own, e_got, gathered)
+
+    def hessians(layer, e_own, e_got):
+        above = layer + 1
+        return call(
+            hessian_kernel,
+            [SMEM] + [VMEM] * 9,
+            [slot, slot, slot, cut, cut] * 2,
+            [],
+            2 * work,
+            6 << 20,
+        )(
+            place,
+            *(states[layer], cots[layer], fulls[layer], e_own, e_got),
+            *(states[above], cots[above], fulls[above], e_fulls[above]),
+        )
+
+    def first_step(blocks):
+        return (
+            shift(blocks[3], "z", 1),
+            shift(blocks[4], "z", -1),
+            shift(blocks[8], "x", 1),
+            shift(blocks[9], "x", -1),
+        )
+
+    def added(blocks, got):
+        return call(step_kernel, [VMEM] * 8, [slot] * 4, moved=5 << 20)(
+            *(blocks[1], blocks[2], got[0], got[1]), *(blocks[6], blocks[7], got[2], got[3])
+        )
+
+    def second_step(blocks, sent):
+        down_parts.extend([blocks[0], shift(sent[0], "z", 1), shift(sent[1], "z", -1)])
+        up_parts.extend([blocks[5], shift(sent[2], "x", 1), shift(sent[3], "x", -1)])
+
+    cots[3] = cot
+    cot, part, e_fulls[3] = backward(3, cot, part, swap(part))
+    cots[2] = cot
+    e_own, e_got = part, swap(part)
+    blocks = hessians(2, e_own, e_got)
+    cot, blocks = lax.optimization_barrier((cot, blocks))
+    got = first_step(blocks)
+    cot, part, e_fulls[2] = backward(2, cot, e_own, e_got)
+    cots[1] = cot
+    e_own, e_got = part, swap(part)
+    sent = added(blocks, got)
+    cot, sent = lax.optimization_barrier((cot, sent))
+    second_step(blocks, sent)
+    cot, part, e_fulls[1] = backward(1, cot, e_own, e_got)
+    cots[0] = cot
+    blocks = hessians(0, part, swap(part))
+    blocks, down_parts, up_parts = lax.optimization_barrier((blocks, down_parts, up_parts))
+    second_step(blocks, added(blocks, first_step(blocks)))
 
     four = shape((LAYERS, 128, RANK), BF16)
-    downs = call(ring_kernel, [VMEM] * 8, [four] * 4, moved=5 << 20)(*down_parts)
+    downs = call(ring_kernel, [VMEM] * 6, [four] * 4, moved=5 << 20)(*down_parts)
     downs = received(downs, "x")
-    ups = call(ring_kernel, [VMEM] * 8, [four] * 4, moved=5 << 20)(*up_parts)
+    ups = call(ring_kernel, [VMEM] * 6, [four] * 4, moved=5 << 20)(*up_parts)
     ups = received(ups, "z")
     blocks = call(
         layer_kernel, [SMEM] + [VMEM] * 8, [shape((256, RANK), BF16)] * 4, moved=2 << 20
@@ -426,9 +477,10 @@
     share, totals = call(
         totals_kernel,
         [VMEM] * 6,
-        [shape((256, RANK), F32), shape((8, 128), F32)],
+        [shape((256, RANK), F32), shape((1, 128), F32)],
     )(*received(blocks, "y"), gain, jnp.concatenate([down_vector[0], up_vector[0].T], 0))
-    totals = sum_all(totals)
+    totals = jnp.broadcast_to(totals[None], (128, 1, 128))
+    totals = lax.all_to_all(totals, ("y", "z", "x", "c"), 0, 0).reshape(128, 128)
     next_down, next_up, quotient = call(
         output_kernel,
         [VMEM] * 2,

time: 293 us -> 261 us (0.89); the launches traced: 289 us -> 260 us
  waiting for transfers between devices: 167 us -> 137 us
  blocking collectives: 0 us -> 21.6 us
  starting transfers between devices: 60.4 us -> 39.9 us
    ppermute x30 -> x25, waiting for transfers between devices: 57.4 us -> 26.1 us  [shift(): return lax.ppermute(value, axis, [(i, (i + steps) % 4) for i in range(4)])]
    all_to_all x0 -> x1, blocking collectives: none -> 21.6 us  [local(): lax.all_to_all(totals, ('y', 'z', 'x', 'c'), 0, 0).reshape(128, 128)]
    ppermute x30 -> x25, starting transfers between devices: 46.6 us -> 31.7 us  [shift(): return lax.ppermute(value, axis, [(i, (i + steps) % 4) for i in range(4)])]
    ppermute x11 -> x10, starting transfers between devices: 13.7 us -> 8.18 us  [swap(): return lax.ppermute(value, 'c', [(0, 1), (1, 0)])]
    ppermute x11 -> x10, waiting for transfers between devices: 7 us -> 8.15 us  [swap(): return lax.ppermute(value, 'c', [(0, 1), (1, 0)])]
    pallas_call x8 -> x10, Pallas kernels: 17.9 us -> 18.2 us  [the longest x3 12.1 us: backward(): call(functools.partial(backward_kernel, layer), [VMEM] * 5 + [ANY], [wide...]
  transfers between devices with their start and end apart: 42 -> 36, of which waited for: 24 -> 19; matrix products, arithmetic and copies ran while one was open for 2% -> 2% of each run, Pallas kernels for 5% -> 6%
where the time goes in v2:
time: 261 us; the launch traced here: 260 us
  waiting for transfers between devices  137 us (52%)
  starting transfers between devices  39.9 us (15%)
  Pallas kernels  35.3 us (14%)
  blocking collectives  21.6 us (8%)
  between operations  14.4 us (6%)
  local copies, waits for them, and re-layouts  9.79 us (4%)
  other arithmetic  2.65 us (1%)
    all_gather x1, waiting for transfers between devices, local(): gathered = lax.all_gather(chunk, ('y', 'z', 'x'), axis=0, tiled=True)  102 us
    ppermute x25, starting transfers between devices, shift(): return lax.ppermute(value, axis, [(i, (i + steps) % 4) for i in range(4)])  31.7 us
    ppermute x25, waiting for transfers between devices, shift(): return lax.ppermute(value, axis, [(i, (i + steps) % 4) for i in range(4)])  26.1 us
    all_to_all x1, blocking collectives, local(): lax.all_to_all(totals, ('y', 'z', 'x', 'c'), 0, 0).reshape(128, 128)  21.6 us
    pallas_call x3, Pallas kernels, backward(): call(functools.partial(backward_kernel, layer), [VMEM] * 5 + [ANY], [wide...  12.1 us
    pallas_call x3, Pallas kernels, local(): call(functools.partial(forward_kernel, layer), [VMEM, VMEM, VMEM, ANY], [...  10.8 us
    ppermute x10, starting transfers between devices, swap(): return lax.ppermute(value, 'c', [(0, 1), (1, 0)])  8.18 us
    ppermute x10, waiting for transfers between devices, swap(): return lax.ppermute(value, 'c', [(0, 1), (1, 0)])  8.15 us
  transfers between devices with their start and end apart: 36, of which 19 were waited for; matrix products, arithmetic and copies ran while one was open for 2% of the time, Pallas kernels for 6%

profile of v2, /device:TPU:1, one launch (start us, length us, event | category | flops | bytes accessed | tf_op | source)
XLA Modules:
  0.0 260.3 jit_solution(5516770601824930158)
XLA Ops:
  17.0 102.3 %all-gather.3.cloned.1.call-done = bf16[256,128,256]{2,1,0:T(8,128)(2,1)} async-done(((bf16[4,128,256]{2,1,0:T(8,128)(2,1)}), bf16[256,128,256]{2,1,0:T(8,128)(2,1)}) %all-gather.3.cloned.1.call-update) | async-done | bytes 16777232 | tf_op jit(solution)/shard_map/all_gather | solution.py:368
  122.8 3.6 %shard_map.95 = (bf16[128,2048]{1,0:T(8,128)(2,1)S(1)}, f32[64,640]{1,0:T(8,128)S(1)}, f32[64,640]{1,0:T(8,128)S(1)}) custom-call(bf16[128,2048]{1,0:T(8,128)(2,1)S(1)} %maximum_maximum_fusion.x_ref.refs_0_, f32[64,640]{1,0:T(8,128)S(1)} %shard_map.94.own_ref, f32[64,640]{1,0:T(8,128)S(1)} %collective-permute-done.1.got_ref, ...), custom_call_target="tpu_custom_call" | custom-call | flops 402653184 | bytes 5242880 | tf_op jit(solution)/shard_map/pallas_call | solution.py:385
  128.8 3.6 %shard_map.96 = (bf16[128,2048]{1,0:T(8,128)(2,1)S(1)}, f32[64,640]{1,0:T(8,128)S(1)}, f32[64,640]{1,0:T(8,128)S(1)}) custom-call(bf16[128,2048]{1,0:T(8,128)(2,1)S(1)} %get-tuple-element.100.x_ref.refs_5_, f32[64,640]{1,0:T(8,128)S(1)} %get-tuple-element.101.own_ref, f32[64,640]{1,0:T(8,128)S(1)} %collective-permute-done.2.got_ref, ...), custom_call_target="tpu_custom_call" | custom-call | flops 402653184 | bytes 5242880 | tf_op jit(solution)/shard_map/pallas_call | solution.py:385
  133.9 3.6 %shard_map.97 = (bf16[128,2048]{1,0:T(8,128)(2,1)S(1)}, f32[64,640]{1,0:T(8,128)S(1)}, f32[64,640]{1,0:T(8,128)S(1)}) custom-call(bf16[128,2048]{1,0:T(8,128)(2,1)S(1)} %get-tuple-element.102.x_ref.refs_0_, f32[64,640]{1,0:T(8,128)S(1)} %get-tuple-element.103.own_ref, f32[64,640]{1,0:T(8,128)S(1)} %collective-permute-done.3.got_ref, ...), custom_call_target="tpu_custom_call" | custom-call | flops 402653184 | bytes 5242880 | tf_op jit(solution)/shard_map/pallas_call | solution.py:385
  139.0 2.9 %shard_map.98 = (bf16[128,2048]{1,0:T(8,128)(2,1)S(1)}, f32[64,512]{1,0:T(8,128)S(1)}, f32[64,640]{1,0:T(8,128)S(1)}) custom-call(bf16[128,2048]{1,0:T(8,128)(2,1)S(1)} %get-tuple-element.104.x_ref.refs_5_, f32[64,640]{1,0:T(8,128)S(1)} %get-tuple-element.105.own_ref, f32[64,640]{1,0:T(8,128)S(1)} %collective-permute-done.4.got_ref, ...), custom_call_target="tpu_custom_call" | custom-call | flops 402653184 | bytes 3145728 | tf_op jit(solution)/shard_map/pallas_call | solution.py:395
  143.6 4.0 %shard_map.99 = (bf16[128,2048]{1,0:T(8,128)(2,1)S(1)}, f32[64,512]{1,0:T(8,128)}, f32[64,512]{1,0:T(8,128)S(1)}) custom-call(bf16[128,2048]{1,0:T(8,128)(2,1)S(1)} %get-tuple-element.104.x_ref.refs_5_, bf16[128,2048]{1,0:T(8,128)(2,1)S(1)} %get-tuple-element.106.cot_ref.refs_6_, f32[64,640]{1,0:T(8,128)S(1)} %get-tuple-element.107.full_ref.refs_7_, ...), custom_call_target="tpu_custom_call" | custom-call | flops 402653184 | bytes 5242880 | tf_op jit(solution)/shard_map/pallas_call | solution.py:409
  152.4 2.5 shard_map.100
  160.4 4.7 %shard_map.101 = (bf16[128,2048]{1,0:T(8,128)(2,1)S(1)}, f32[64,512]{1,0:T(8,128)S(1)}, f32[64,512]{1,0:T(8,128)}) custom-call(bf16[128,2048]{1,0:T(8,128)(2,1)S(1)} %get-tuple-element.102.x_ref.refs_0_, bf16[128,2048]{1,0:T(8,128)(2,1)S(1)} %get-tuple-element.123.refs_1_.cot_ref, f32[64,640]{1,0:T(8,128)S(1)} %get-tuple-element.110.refs_2_.full_ref, ...), custom_call_target="tpu_custom_call" | custom-call | flops 402653184 | bytes 5242880 | tf_op jit(solution)/shard_map/pallas_call | solution.py:409
  166.2 2.7 %collective-permute-start.15 = (bf16[4,2,128,256]{3,2,1,0:T(8,128)(2,1)S(1)}, bf16[4,2,128,256]{3,2,1,0:T(8,128)(2,1)S(1)}, u32[]{:S(2)}, u32[]{:S(2)}) collective-permute-start(bf16[4,2,128,256]{3,2,1,0:T(8,128)(2,1)S(1)} %get-tuple-element.156), channel_id=1, source_target_pairs={{0,24},{8,0},{16,8},{24,16},{1,25},{9,1},{17,9},{25,17},{2,26},{10... | collective-permute-start | bytes 1572872 | tf_op jit(solution)/shard_map/ppermute | solution.py:22
  171.5 2.9 %collective-permute-start.12 = (f32[64,512]{1,0:T(8,128)S(1)}, f32[64,512]{1,0:T(8,128)S(1)}, u32[]{:S(2)}, u32[]{:S(2)}) collective-permute-start(f32[64,512]{1,0:T(8,128)S(1)} %get-tuple-element.139.e_own_ref), channel_id=1, source_target_pairs={{0,1},{1,0},{2,3},{3,2},{4,5},{5,4},{6,7},{7,6},{8,9},{9,8},{10,11... | collective-permute-start | bytes 393224 | tf_op jit(solution)/shard_map/ppermute | solution.py:26
  175.5 3.4 %shard_map.103 = (bf16[128,2048]{1,0:T(8,128)(2,1)S(1)}, f32[64,512]{1,0:T(8,128)S(1)}, f32[64,512]{1,0:T(8,128)S(1)}) custom-call(bf16[128,2048]{1,0:T(8,128)(2,1)S(1)} %get-tuple-element.100.x_ref.refs_5_, bf16[128,2048]{1,0:T(8,128)(2,1)S(1)} %get-tuple-element.137.cot_ref.refs_6_, f32[64,640]{1,0:T(8,128)S(1)} %get-tuple-element.138.full_ref.refs_7_, ...), custom_call_target="tpu_custom_call" | custom-call | flops 402653184 | bytes 5242880 | tf_op jit(solution)/shard_map/pallas_call | solution.py:409
  182.5 2.7 %collective-permute-start.19 = (bf16[2,2,128,256]{3,2,1,0:T(8,128)(2,1)S(1)}, bf16[2,2,128,256]{3,2,1,0:T(8,128)(2,1)S(1)}, u32[]{:S(2)}, u32[]{:S(2)}) collective-permute-start(bf16[2,2,128,256]{3,2,1,0:T(8,128)(2,1)S(1)} %get-tuple-element.167), channel_id=1, source_target_pairs={{0,24},{8,0},{16,8},{24,16},{1,25},{9,1},{17,9},{25,17},{2,26},{10... | collective-permute-start | bytes 786440 | tf_op jit(solution)/shard_map/ppermute | solution.py:22
  185.2 2.7 %collective-permute-start.21 = (bf16[2,2,128,256]{3,2,1,0:T(8,128)(2,1)S(1)}, bf16[2,2,128,256]{3,2,1,0:T(8,128)(2,1)S(1)}, u32[]{:S(2)}, u32[]{:S(2)}) collective-permute-start(bf16[2,2,128,256]{3,2,1,0:T(8,128)(2,1)S(1)} %get-tuple-element.171), channel_id=1, source_target_pairs={{0,6},{2,0},{4,2},{6,4},{1,7},{3,1},{5,3},{7,5},{8,14},{10,8},{12,... | collective-permute-start | bytes 786440 | tf_op jit(solution)/shard_map/ppermute | solution.py:22
  189.6 2.3 collective-permute-done.20.refs_6_
  192.3 2.7 %collective-permute-start.23 = (bf16[4,2,128,256]{3,2,1,0:T(8,128)(2,1)S(1)}, bf16[4,2,128,256]{3,2,1,0:T(8,128)(2,1)S(1)}, u32[]{:S(2)}, u32[]{:S(2)}) collective-permute-start(bf16[4,2,128,256]{3,2,1,0:T(8,128)(2,1)S(1)} %get-tuple-element.173), channel_id=1, source_target_pairs={{0,24},{8,0},{16,8},{24,16},{1,25},{9,1},{17,9},{25,17},{2,26},{10... | collective-permute-start | bytes 1572872 | tf_op jit(solution)/shard_map/ppermute | solution.py:22
  194.9 2.7 %collective-permute-start.28 = (bf16[4,2,128,256]{3,2,1,0:T(8,128)(2,1)S(1)}, bf16[4,2,128,256]{3,2,1,0:T(8,128)(2,1)S(1)}, u32[]{:S(2)}, u32[]{:S(2)}) collective-permute-start(bf16[4,2,128,256]{3,2,1,0:T(8,128)(2,1)S(1)} %get-tuple-element.183), channel_id=1, source_target_pairs={{0,6},{2,0},{4,2},{6,4},{1,7},{3,1},{5,3},{7,5},{8,14},{10,8},{12,... | collective-permute-start | bytes 1572872 | tf_op jit(solution)/shard_map/ppermute | solution.py:22
  197.6 5.9 %collective-permute-done.22.refs_4_ = bf16[4,2,128,256]{3,2,1,0:T(8,128)(2,1)S(1)} collective-permute-done((bf16[4,2,128,256]{3,2,1,0:T(8,128)(2,1)S(1)}, bf16[4,2,128,256]{3,2,1,0:T(8,128)(2,1)S(1)}, u32[]{:S(2)}, u32[]{:S(2)}) %collective-permute-start.22) | collective-permute-done | bytes 524320 | tf_op jit(solution)/shard_map/ppermute | solution.py:22
  204.0 2.7 %collective-permute-start.25 = (bf16[4,128,256]{2,1,0:T(8,128)(2,1)S(1)}, bf16[4,128,256]{2,1,0:T(8,128)(2,1)S(1)}, u32[]{:S(2)}, u32[]{:S(2)}) collective-permute-start(bf16[4,128,256]{2,1,0:T(8,128)(2,1)S(1)} %get-tuple-element.176), channel_id=1, source_target_pairs={{0,6},{2,0},{4,2},{6,4},{1,7},{3,1},{5,3},{7,5},{8,14},{10,8},{12,... | collective-permute-start | bytes 786440 | tf_op jit(solution)/shard_map/ppermute | solution.py:22
  207.5 2.7 %collective-permute-start.30 = (bf16[4,128,256]{2,1,0:T(8,128)(2,1)S(1)}, bf16[4,128,256]{2,1,0:T(8,128)(2,1)S(1)}, u32[]{:S(2)}, u32[]{:S(2)}) collective-permute-start(bf16[4,128,256]{2,1,0:T(8,128)(2,1)S(1)} %get-tuple-element.186), channel_id=1, source_target_pairs={{0,24},{8,0},{16,8},{24,16},{1,25},{9,1},{17,9},{25,17},{2,26},{10... | collective-permute-start | bytes 786440 | tf_op jit(solution)/shard_map/ppermute | solution.py:22
  210.1 3.0 %collective-permute-done.24.refs_1_ = bf16[4,128,256]{2,1,0:T(8,128)(2,1)S(1)} collective-permute-done((bf16[4,128,256]{2,1,0:T(8,128)(2,1)S(1)}, bf16[4,128,256]{2,1,0:T(8,128)(2,1)S(1)}, u32[]{:S(2)}, u32[]{:S(2)}) %collective-permute-start.24) | collective-permute-done | bytes 262176 | tf_op jit(solution)/shard_map/ppermute | solution.py:22
  213.8 5.7 %collective-permute-done.26.refs_3_ = bf16[4,128,256]{2,1,0:T(8,128)(2,1)S(1)} collective-permute-done((bf16[4,128,256]{2,1,0:T(8,128)(2,1)S(1)}, bf16[4,128,256]{2,1,0:T(8,128)(2,1)S(1)}, u32[]{:S(2)}, u32[]{:S(2)}) %collective-permute-start.26) | collective-permute-done | bytes 262176 | tf_op jit(solution)/shard_map/ppermute | solution.py:22
  219.5 2.3 collective-permute-done.31.refs_7_
  227.7 3.0 %collective-permute-done.34.b3 = bf16[256,256]{1,0:T(8,128)(2,1)S(1)} collective-permute-done((bf16[256,256]{1,0:T(8,128)(2,1)S(1)}, bf16[256,256]{1,0:T(8,128)(2,1)S(1)}, u32[]{:S(2)}, u32[]{:S(2)}) %collective-permute-start.34) | collective-permute-done | bytes 131104 | tf_op jit(solution)/shard_map/ppermute | solution.py:22
  230.9 21.6 %all_to_all.5 = f32[128,1,128]{2,1,0:T(1,128)S(1)} all-to-all(f32[128,1,128]{2,1,0:T(1,128)S(1)} %broadcast_in_dim.24), channel_id=1, replica_groups=mesh['y'=4,'z'=4,'x'=4,'c'=2] {'y','z','x','c'}, dimensions={0} | all-to-all | bytes 131072 | tf_op jit(solution)/shard_map/all_to_all | solution.py:483
  (103 shorter events, 49.8 us)
Async XLA Ops:
  7.2 112.1 %all-gather.3.cloned.1.call-start = ((), (), s32[]{:S(2)}) async-start(), calls=%async_computation.1 | async-start | bytes 17039360 | tf_op jit(solution)/shard_map/all_gather | solution.py:368
  155.0 10.1 %collective-permute-start.8 = (bf16[2,2,128,256]{3,2,1,0:T(8,128)(2,1)S(1)}, bf16[2,2,128,256]{3,2,1,0:T(8,128)(2,1)S(1)}, u32[]{:S(2)}, u32[]{:S(2)}) collective-permute-start(bf16[2,2,128,256]{3,2,1,0:T(8,128)(2,1)S(1)} %get-tuple-element.127), channel_id=1, source_target_pairs={{0,8},{8,16},{16,24},{24,0},{1,9},{9,17},{17,25},{25,1},{2,10},{10... | collective-permute-start | bytes 786440 | tf_op jit(solution)/shard_map/ppermute | solution.py:22
  155.6 9.5 %collective-permute-start.9 = (bf16[2,2,128,256]{3,2,1,0:T(8,128)(2,1)S(1)}, bf16[2,2,128,256]{3,2,1,0:T(8,128)(2,1)S(1)}, u32[]{:S(2)}, u32[]{:S(2)}) collective-permute-start(bf16[2,2,128,256]{3,2,1,0:T(8,128)(2,1)S(1)} %get-tuple-element.128), channel_id=1, source_target_pairs={{0,24},{8,0},{16,8},{24,16},{1,25},{9,1},{17,9},{25,17},{2,26},{10... | collective-permute-start | bytes 786440 | tf_op jit(solution)/shard_map/ppermute | solution.py:22
  157.7 8.1 %collective-permute-start.10 = (bf16[2,2,128,256]{3,2,1,0:T(8,128)(2,1)S(1)}, bf16[2,2,128,256]{3,2,1,0:T(8,128)(2,1)S(1)}, u32[]{:S(2)}, u32[]{:S(2)}) collective-permute-start(bf16[2,2,128,256]{3,2,1,0:T(8,128)(2,1)S(1)} %get-tuple-element.131), channel_id=1, source_target_pairs={{0,2},{2,4},{4,6},{6,0},{1,3},{3,5},{5,7},{7,1},{8,10},{10,12},{12... | collective-permute-start | bytes 786440 | tf_op jit(solution)/shard_map/ppermute | solution.py:22
  158.9 6.9 %collective-permute-start.11 = (bf16[2,2,128,256]{3,2,1,0:T(8,128)(2,1)S(1)}, bf16[2,2,128,256]{3,2,1,0:T(8,128)(2,1)S(1)}, u32[]{:S(2)}, u32[]{:S(2)}) collective-permute-start(bf16[2,2,128,256]{3,2,1,0:T(8,128)(2,1)S(1)} %get-tuple-element.132), channel_id=1, source_target_pairs={{0,6},{2,0},{4,2},{6,4},{1,7},{3,1},{5,3},{7,5},{8,14},{10,8},{12,... | collective-permute-start | bytes 786440 | tf_op jit(solution)/shard_map/ppermute | solution.py:22
  166.1 16.3 %collective-permute-start.14 = (bf16[4,2,128,256]{3,2,1,0:T(8,128)(2,1)S(1)}, bf16[4,2,128,256]{3,2,1,0:T(8,128)(2,1)S(1)}, u32[]{:S(2)}, u32[]{:S(2)}) collective-permute-start(bf16[4,2,128,256]{3,2,1,0:T(8,128)(2,1)S(1)} %get-tuple-element.155), channel_id=1, source_target_pairs={{0,8},{8,16},{16,24},{24,0},{1,9},{9,17},{17,25},{25,1},{2,10},{10... | collective-permute-start | bytes 1572872 | tf_op jit(solution)/shard_map/ppermute | solution.py:22
  166.2 16.2 %collective-permute-start.15 = (bf16[4,2,128,256]{3,2,1,0:T(8,128)(2,1)S(1)}, bf16[4,2,128,256]{3,2,1,0:T(8,128)(2,1)S(1)}, u32[]{:S(2)}, u32[]{:S(2)}) collective-permute-start(bf16[4,2,128,256]{3,2,1,0:T(8,128)(2,1)S(1)} %get-tuple-element.156), channel_id=1, source_target_pairs={{0,24},{8,0},{16,8},{24,16},{1,25},{9,1},{17,9},{25,17},{2,26},{10... | collective-permute-start | bytes 1572872 | tf_op jit(solution)/shard_map/ppermute | solution.py:22
  168.8 13.5 %collective-permute-start.16 = (bf16[4,2,128,256]{3,2,1,0:T(8,128)(2,1)S(1)}, bf16[4,2,128,256]{3,2,1,0:T(8,128)(2,1)S(1)}, u32[]{:S(2)}, u32[]{:S(2)}) collective-permute-start(bf16[4,2,128,256]{3,2,1,0:T(8,128)(2,1)S(1)} %get-tuple-element.158), channel_id=1, source_target_pairs={{0,2},{2,4},{4,6},{6,0},{1,3},{3,5},{5,7},{7,1},{8,10},{10,12},{12... | collective-permute-start | bytes 1572872 | tf_op jit(solution)/shard_map/ppermute | solution.py:22
  169.7 12.7 %collective-permute-start.17 = (bf16[4,2,128,256]{3,2,1,0:T(8,128)(2,1)S(1)}, bf16[4,2,128,256]{3,2,1,0:T(8,128)(2,1)S(1)}, u32[]{:S(2)}, u32[]{:S(2)}) collective-permute-start(bf16[4,2,128,256]{3,2,1,0:T(8,128)(2,1)S(1)} %get-tuple-element.159), channel_id=1, source_target_pairs={{0,6},{2,0},{4,2},{6,4},{1,7},{3,1},{5,3},{7,5},{8,14},{10,8},{12,... | collective-permute-start | bytes 1572872 | tf_op jit(solution)/shard_map/ppermute | solution.py:22
  182.4 7.1 %collective-permute-start.18 = (bf16[2,2,128,256]{3,2,1,0:T(8,128)(2,1)S(1)}, bf16[2,2,128,256]{3,2,1,0:T(8,128)(2,1)S(1)}, u32[]{:S(2)}, u32[]{:S(2)}) collective-permute-start(bf16[2,2,128,256]{3,2,1,0:T(8,128)(2,1)S(1)} %get-tuple-element.166), channel_id=1, source_target_pairs={{0,8},{8,16},{16,24},{24,0},{1,9},{9,17},{17,25},{25,1},{2,10},{10... | collective-permute-start | bytes 786440 | tf_op jit(solution)/shard_map/ppermute | solution.py:22
  182.5 7.1 %collective-permute-start.19 = (bf16[2,2,128,256]{3,2,1,0:T(8,128)(2,1)S(1)}, bf16[2,2,128,256]{3,2,1,0:T(8,128)(2,1)S(1)}, u32[]{:S(2)}, u32[]{:S(2)}) collective-permute-start(bf16[2,2,128,256]{3,2,1,0:T(8,128)(2,1)S(1)} %get-tuple-element.167), channel_id=1, source_target_pairs={{0,24},{8,0},{16,8},{24,16},{1,25},{9,1},{17,9},{25,17},{2,26},{10... | collective-permute-start | bytes 786440 | tf_op jit(solution)/shard_map/ppermute | solution.py:22
  185.1 6.7 %collective-permute-start.20 = (bf16[2,2,128,256]{3,2,1,0:T(8,128)(2,1)S(1)}, bf16[2,2,128,256]{3,2,1,0:T(8,128)(2,1)S(1)}, u32[]{:S(2)}, u32[]{:S(2)}) collective-permute-start(bf16[2,2,128,256]{3,2,1,0:T(8,128)(2,1)S(1)} %get-tuple-element.170), channel_id=1, source_target_pairs={{0,2},{2,4},{4,6},{6,0},{1,3},{3,5},{5,7},{7,1},{8,10},{10,12},{12... | collective-permute-start | bytes 786440 | tf_op jit(solution)/shard_map/ppermute | solution.py:22
  185.2 6.7 %collective-permute-start.21 = (bf16[2,2,128,256]{3,2,1,0:T(8,128)(2,1)S(1)}, bf16[2,2,128,256]{3,2,1,0:T(8,128)(2,1)S(1)}, u32[]{:S(2)}, u32[]{:S(2)}) collective-permute-start(bf16[2,2,128,256]{3,2,1,0:T(8,128)(2,1)S(1)} %get-tuple-element.171), channel_id=1, source_target_pairs={{0,6},{2,0},{4,2},{6,4},{1,7},{3,1},{5,3},{7,5},{8,14},{10,8},{12,... | collective-permute-start | bytes 786440 | tf_op jit(solution)/shard_map/ppermute | solution.py:22
  192.2 11.4 %collective-permute-start.22 = (bf16[4,2,128,256]{3,2,1,0:T(8,128)(2,1)S(1)}, bf16[4,2,128,256]{3,2,1,0:T(8,128)(2,1)S(1)}, u32[]{:S(2)}, u32[]{:S(2)}) collective-permute-start(bf16[4,2,128,256]{3,2,1,0:T(8,128)(2,1)S(1)} %get-tuple-element.172), channel_id=1, source_target_pairs={{0,8},{8,16},{16,24},{24,0},{1,9},{9,17},{17,25},{25,1},{2,10},{10... | collective-permute-start | bytes 1572872 | tf_op jit(solution)/shard_map/ppermute | solution.py:22
  192.3 11.3 %collective-permute-start.23 = (bf16[4,2,128,256]{3,2,1,0:T(8,128)(2,1)S(1)}, bf16[4,2,128,256]{3,2,1,0:T(8,128)(2,1)S(1)}, u32[]{:S(2)}, u32[]{:S(2)}) collective-permute-start(bf16[4,2,128,256]{3,2,1,0:T(8,128)(2,1)S(1)} %get-tuple-element.173), channel_id=1, source_target_pairs={{0,24},{8,0},{16,8},{24,16},{1,25},{9,1},{17,9},{25,17},{2,26},{10... | collective-permute-start | bytes 1572872 | tf_op jit(solution)/shard_map/ppermute | solution.py:22
  194.9 12.1 %collective-permute-start.27 = (bf16[4,2,128,256]{3,2,1,0:T(8,128)(2,1)S(1)}, bf16[4,2,128,256]{3,2,1,0:T(8,128)(2,1)S(1)}, u32[]{:S(2)}, u32[]{:S(2)}) collective-permute-start(bf16[4,2,128,256]{3,2,1,0:T(8,128)(2,1)S(1)} %get-tuple-element.182), channel_id=1, source_target_pairs={{0,2},{2,4},{4,6},{6,0},{1,3},{3,5},{5,7},{7,1},{8,10},{10,12},{12... | collective-permute-start | bytes 1572872 | tf_op jit(solution)/shard_map/ppermute | solution.py:22
  194.9 12.1 %collective-permute-start.28 = (bf16[4,2,128,256]{3,2,1,0:T(8,128)(2,1)S(1)}, bf16[4,2,128,256]{3,2,1,0:T(8,128)(2,1)S(1)}, u32[]{:S(2)}, u32[]{:S(2)}) collective-permute-start(bf16[4,2,128,256]{3,2,1,0:T(8,128)(2,1)S(1)} %get-tuple-element.183), channel_id=1, source_target_pairs={{0,6},{2,0},{4,2},{6,4},{1,7},{3,1},{5,3},{7,5},{8,14},{10,8},{12,... | collective-permute-start | bytes 1572872 | tf_op jit(solution)/shard_map/ppermute | solution.py:22
  203.9 9.2 %collective-permute-start.24 = (bf16[4,128,256]{2,1,0:T(8,128)(2,1)S(1)}, bf16[4,128,256]{2,1,0:T(8,128)(2,1)S(1)}, u32[]{:S(2)}, u32[]{:S(2)}) collective-permute-start(bf16[4,128,256]{2,1,0:T(8,128)(2,1)S(1)} %get-tuple-element.175), channel_id=1, source_target_pairs={{0,2},{2,4},{4,6},{6,0},{1,3},{3,5},{5,7},{7,1},{8,10},{10,12},{12... | collective-permute-start | bytes 786440 | tf_op jit(solution)/shard_map/ppermute | solution.py:22
  204.0 9.8 %collective-permute-start.25 = (bf16[4,128,256]{2,1,0:T(8,128)(2,1)S(1)}, bf16[4,128,256]{2,1,0:T(8,128)(2,1)S(1)}, u32[]{:S(2)}, u32[]{:S(2)}) collective-permute-start(bf16[4,128,256]{2,1,0:T(8,128)(2,1)S(1)} %get-tuple-element.176), channel_id=1, source_target_pairs={{0,6},{2,0},{4,2},{6,4},{1,7},{3,1},{5,3},{7,5},{8,14},{10,8},{12,... | collective-permute-start | bytes 786440 | tf_op jit(solution)/shard_map/ppermute | solution.py:22
  206.7 12.9 %collective-permute-start.26 = (bf16[4,128,256]{2,1,0:T(8,128)(2,1)S(1)}, bf16[4,128,256]{2,1,0:T(8,128)(2,1)S(1)}, u32[]{:S(2)}, u32[]{:S(2)}) collective-permute-start(bf16[4,128,256]{2,1,0:T(8,128)(2,1)S(1)} %get-tuple-element.177), channel_id=1, source_target_pairs={{0,4},{2,6},{4,0},{6,2},{1,5},{3,7},{5,1},{7,3},{8,12},{10,14},{12... | collective-permute-start | bytes 786440 | tf_op jit(solution)/shard_map/ppermute | solution.py:22
  207.4 12.2 %collective-permute-start.29 = (bf16[4,128,256]{2,1,0:T(8,128)(2,1)S(1)}, bf16[4,128,256]{2,1,0:T(8,128)(2,1)S(1)}, u32[]{:S(2)}, u32[]{:S(2)}) collective-permute-start(bf16[4,128,256]{2,1,0:T(8,128)(2,1)S(1)} %get-tuple-element.185), channel_id=1, source_target_pairs={{0,8},{8,16},{16,24},{24,0},{1,9},{9,17},{17,25},{25,1},{2,10},{10... | collective-permute-start | bytes 786440 | tf_op jit(solution)/shard_map/ppermute | solution.py:22
  207.5 12.1 %collective-permute-start.30 = (bf16[4,128,256]{2,1,0:T(8,128)(2,1)S(1)}, bf16[4,128,256]{2,1,0:T(8,128)(2,1)S(1)}, u32[]{:S(2)}, u32[]{:S(2)}) collective-permute-start(bf16[4,128,256]{2,1,0:T(8,128)(2,1)S(1)} %get-tuple-element.186), channel_id=1, source_target_pairs={{0,24},{8,0},{16,8},{24,16},{1,25},{9,1},{17,9},{25,17},{2,26},{10... | collective-permute-start | bytes 786440 | tf_op jit(solution)/shard_map/ppermute | solution.py:22
  213.1 8.7 %collective-permute-start.31 = (bf16[4,128,256]{2,1,0:T(8,128)(2,1)S(1)}, bf16[4,128,256]{2,1,0:T(8,128)(2,1)S(1)}, u32[]{:S(2)}, u32[]{:S(2)}) collective-permute-start(bf16[4,128,256]{2,1,0:T(8,128)(2,1)S(1)} %get-tuple-element.187), channel_id=1, source_target_pairs={{0,16},{8,24},{16,0},{24,8},{1,17},{9,25},{17,1},{25,9},{2,18},{10... | collective-permute-start | bytes 786440 | tf_op jit(solution)/shard_map/ppermute | solution.py:22
  225.4 5.3 %collective-permute-start.34 = (bf16[256,256]{1,0:T(8,128)(2,1)S(1)}, bf16[256,256]{1,0:T(8,128)(2,1)S(1)}, u32[]{:S(2)}, u32[]{:S(2)}) collective-permute-start(bf16[256,256]{1,0:T(8,128)(2,1)S(1)} %get-tuple-element.191), channel_id=1, source_target_pairs={{0,64},{32,96},{64,0},{96,32},{1,65},{33,97},{65,1},{97,33},{2,66}... | collective-permute-start | bytes 393224 | tf_op jit(solution)/shard_map/ppermute | solution.py:22
  (19 other events, 123.4 us)
Sparse Core Ops, SparseCore 0:
  11.6 107.5 all-gather.2
